TPU v7x, 32 devices: a whole 2x2x4 slice. The times are simulated.
32 devices in a mesh: node: 8 (over z, x), local: 4 (over y, core).
Axes of the slice: x: 2, y: 2, z: 4, core: 2. Of those that a mesh axis runs over, the one named last changes fastest.
Arguments:
- tokens: bfloat16 [128, 4096], P('node', 'local'), may hold values from -6 to 6
- sign_bits: int32 [4096], P('local'), may hold values 0 or 1
- routes: int32 [128, 4], P('node'), may hold values from 0 to 7, all different within a row; in each aligned block of 16 rows (0 to 15, 16 to 31, ...) at most 16 rows name the same one
- gate_values: float32 [128, 4], P('node'), may hold values from 0.1 to 1
- gate_w: bfloat16 [8, 4096, 1024], P('node', 'local'), may hold values from -0.09375 to 0.09375
- up_w: bfloat16 [8, 4096, 1024], P('node', 'local'), may hold values from -0.09375 to 0.09375
- down_w: bfloat16 [8, 1024, 4096], P('node', None, 'local'), may hold values from -0.1875 to 0.1875
Outputs:
- mixed: bfloat16 [128, 4096], P('node', 'local')
Inputs may be any that keep to these rules, and one draw needn't show every extreme that they name: `routes`: each row names 4 different experts; within the rows of one index of node (16 tokens, aligned blocks) no expert is named by more than 16 rows.
All inputs are finite; a program needn't handle non-finite values. No bound on the sum of `sign_bits` on one device may be relied on, other than what follows from the above.
Results may differ from a plain program's by a relative error of at most 0.0071.
Values may be sent and summed in bfloat16 or wider, within the bound.
A program may use at most 64 MiB of HBM per device.

v0:
```python
import math

import jax
import jax.numpy as jnp
from jax import lax
from jax.sharding import PartitionSpec as P

HB = 128


def hadamard_table(block_order):
    kernel_two = jnp.array([[1.0, 1.0], [1.0, -1.0]], jnp.float32)
    matrix = jnp.ones((1, 1), jnp.float32)
    while matrix.shape[0] < block_order:
        matrix = jnp.kron(matrix, kernel_two)
    return matrix / math.sqrt(block_order)


def slot_table(routes, experts, capacity):
    rows_all = routes.shape[0] * routes.shape[1]
    flat_routes = routes.reshape(rows_all)
    onehot = (flat_routes[:, None] == jnp.arange(experts, dtype=jnp.int32)[None, :]).astype(
        jnp.int32
    )
    ranks = jnp.sum(jnp.cumsum(onehot, axis=0) * onehot, axis=1) - 1
    slot_ids = flat_routes * capacity + ranks
    return slot_ids[None, :] == jnp.arange(experts * capacity, dtype=jnp.int32)[:, None]


def per_device(tokens, sign_bits, routes, gate_values, gate_w, up_w, down_w):
    experts = lax.axis_size("node")
    tok_node, width_dev = tokens.shape
    top_count = routes.shape[1]
    capacity = max(2, 2 * tok_node * top_count // experts)
    placed = slot_table(routes, experts, capacity).reshape(experts * capacity, tok_node, top_count)
    scatter_mat = jnp.any(placed, axis=2).astype(jnp.bfloat16)
    combine_mat = jnp.sum(placed.astype(jnp.float32) * gate_values[None, :, :], axis=2)
    hadamard = hadamard_table(HB)
    sign_vals = (1 - 2 * sign_bits).astype(jnp.float32)
    signed = tokens.astype(jnp.float32) * sign_vals[None, :]
    block_count = width_dev // HB
    group_size = min(2, block_count)
    group_width = group_size * HB
    received = []
    for group_index in range(block_count // group_size):
        rotated_parts = []
        for inner_index in range(group_size):
            first_col = group_index * group_width + inner_index * HB
            feature_block = signed[:, first_col : first_col + HB]
            rotated_parts.append(
                jnp.dot(feature_block, hadamard, precision=lax.Precision.HIGHEST).astype(
                    jnp.bfloat16
                )
            )
        rotated = jnp.concatenate(rotated_parts, axis=1)
        outgoing = jnp.dot(scatter_mat, rotated, preferred_element_type=jnp.float32).astype(
            jnp.bfloat16
        )
        received.append(lax.all_to_all(outgoing, "node", split_axis=0, concat_axis=0, tiled=True))
    arrived = jnp.concatenate(received, axis=1)
    gate_part = jnp.dot(arrived, gate_w[0], preferred_element_type=jnp.float32)
    up_part = jnp.dot(arrived, up_w[0], preferred_element_type=jnp.float32)
    gate_full, up_full = lax.psum((gate_part, up_part), "local")
    hidden_full = (jax.nn.silu(gate_full) * up_full).astype(jnp.bfloat16)
    expert_sum = jnp.dot(hidden_full, down_w[0], preferred_element_type=jnp.float32)
    expert_out = expert_sum.astype(jnp.bfloat16)
    combine_left = combine_mat.T
    mixed_blocks = []
    for group_index in range(block_count // group_size):
        out_block = expert_out[:, group_index * group_width : (group_index + 1) * group_width]
        returned_rows = lax.all_to_all(out_block, "node", split_axis=0, concat_axis=0, tiled=True)
        mixed_blocks.append(
            jnp.dot(
                combine_left, returned_rows.astype(jnp.float32), precision=lax.Precision.HIGHEST
            )
        )
    return jnp.concatenate(mixed_blocks, axis=1).astype(jnp.bfloat16)


def solution(mesh):
    in_specs = (
        P("node", "local"),
        P("local"),
        P("node", None),
        P("node", None),
        P("node", "local", None),
        P("node", "local", None),
        P("node", None, "local"),
    )
    out_specs = P("node", "local")
    return jax.shard_map(
        per_device, mesh=mesh, in_specs=in_specs, out_specs=out_specs, check_vma=False
    )
```

profile of v0, /device:TPU:0, one launch (start us, length us, event | category | flops | bytes accessed | tf_op | source)
XLA Modules:
  0.0 154.4 jit_solution(2445655108982102085)
XLA Ops:
  6.5 0.0 copy-start
  6.5 0.9 broadcast_multiply_fusion.4
  7.5 0.1 mul.220
  7.6 0.8 broadcast_multiply_fusion.3
  8.3 0.1 mul.224
  8.4 0.8 broadcast_multiply_fusion.2
  9.1 0.1 mul.228
  9.2 0.8 broadcast_multiply_fusion.1
  10.0 0.1 mul.232
  10.2 0.9 broadcast_multiply_fusion
  11.1 0.6 mul.236
  11.7 2.4 %multiply_multiply_fusion = f32[64,2,64,2]{3,2,1,0:T(8,128)} fusion(f32[2,2]{1,0:T(2,128)S(1)} %copy-done.2, f32[64,64]{1,0:T(8,128)S(1)} %mul.236), kind=kLoop, calls=%fused_computation | loop fusion | flops 32768 | bytes 81936 | tf_op jit(solution)/shard_map/div | solution.py:16
  14.1 4.0 %div.14 = f32[128,128]{1,0:T(8,128)S(1)} reshape(f32[64,2,64,2]{3,2,1,0:T(8,128)} %multiply_multiply_fusion) | data formatting | bytes 131072 | tf_op jit(solution)/shard_map/div | solution.py:16
  18.1 0.0 copy-done.3
  18.1 0.2 convolution_convert_fusion.14
  18.3 0.2 convolution_convert_fusion.15
  18.5 0.0 copy-done.4
  18.5 0.1 copy.18
  18.6 0.1 eq.29
  18.7 0.1 fusion.11
  18.7 0.1 reduce_window_sum.11
  18.8 0.2 select_reduce_fusion.1
  19.0 0.1 sub.13
  19.1 0.1 copy.19
  19.2 0.1 fusion.10
  19.3 0.8 convolution_convert_fusion.3
  20.2 7.3 %all-to-all-start = ((bf16[8,16,256]{2,1,0:T(8,128)(2,1)}), bf16[8,16,256]{2,1,0:T(8,128)(2,1)S(1)}, u32[]{:S(2)}, u32[]{:S(2)}) async-start(bf16[8,16,256]{2,1,0:T(8,128)(2,1)} %bitcast), calls=%async_computation | async-start | bytes 131072 | tf_op jit(solution)/shard_map/all_to_all | solution.py:59
  27.4 0.2 convolution_convert_fusion.12
  27.6 0.2 convolution_convert_fusion.13
  27.7 0.2 convolution_convert_fusion.10
  27.9 0.2 convolution_convert_fusion.11
  28.1 0.2 convolution_convert_fusion.8
  28.3 0.2 convolution_convert_fusion.9
  28.4 0.9 convolution_convert_fusion.2
  29.3 5.0 %all-to-all-done = bf16[8,16,256]{2,1,0:T(8,128)(2,1)S(1)} async-done(((bf16[8,16,256]{2,1,0:T(8,128)(2,1)}), bf16[8,16,256]{2,1,0:T(8,128)(2,1)S(1)}, u32[]{:S(2)}, u32[]{:S(2)}) %all-to-all-start) | async-done | bytes 65568 | tf_op jit(solution)/shard_map/all_to_all | solution.py:59
  34.3 3.3 %all-to-all-start.1 = ((bf16[8,16,256]{2,1,0:T(8,128)(2,1)}), bf16[8,16,256]{2,1,0:T(8,128)(2,1)S(1)}, u32[]{:S(2)}, u32[]{:S(2)}) async-start(bf16[8,16,256]{2,1,0:T(8,128)(2,1)} %bitcast.2), calls=%async_computation.1 | async-start | bytes 131072 | tf_op jit(solution)/shard_map/all_to_all | solution.py:59
  37.7 0.8 convolution_convert_fusion.1
  38.5 6.0 %all-to-all-done.1 = bf16[8,16,256]{2,1,0:T(8,128)(2,1)S(1)} async-done(((bf16[8,16,256]{2,1,0:T(8,128)(2,1)}), bf16[8,16,256]{2,1,0:T(8,128)(2,1)S(1)}, u32[]{:S(2)}, u32[]{:S(2)}) %all-to-all-start.1) | async-done | bytes 65568 | tf_op jit(solution)/shard_map/all_to_all | solution.py:59
  44.5 3.3 %all-to-all-start.2 = ((bf16[8,16,256]{2,1,0:T(8,128)(2,1)}), bf16[8,16,256]{2,1,0:T(8,128)(2,1)S(1)}, u32[]{:S(2)}, u32[]{:S(2)}) async-start(bf16[8,16,256]{2,1,0:T(8,128)(2,1)} %bitcast.4), calls=%async_computation.2 | async-start | bytes 131072 | tf_op jit(solution)/shard_map/all_to_all | solution.py:59
  47.9 0.0 all-reduce.3.cloned.1.call-start
  47.9 0.2 convolution_convert_fusion
  48.1 6.6 %all-to-all-done.2 = bf16[8,16,256]{2,1,0:T(8,128)(2,1)S(1)} async-done(((bf16[8,16,256]{2,1,0:T(8,128)(2,1)}), bf16[8,16,256]{2,1,0:T(8,128)(2,1)S(1)}, u32[]{:S(2)}, u32[]{:S(2)}) %all-to-all-start.2) | async-done | bytes 65568 | tf_op jit(solution)/shard_map/all_to_all | solution.py:59
  54.7 9.4 %all_to_all.96 = bf16[8,16,256]{2,1,0:T(8,128)(2,1)S(1)} all-to-all(bf16[8,16,256]{2,1,0:T(8,128)(2,1)S(1)} %bitcast.67), channel_id=1, replica_groups=mesh['node'=8,'local'=4] {'node'}, dimensions={0} | all-to-all | bytes 131072 | tf_op jit(solution)/shard_map/all_to_all | solution.py:59
  64.1 1.3 fusion.4
  65.4 0.0 copy-done.1
  65.4 1.3 fusion.2
  66.7 0.0 all-reduce.3.cloned.1.call-update
  66.7 33.9 %all-reduce.3.cloned.1.call-done = (f32[128,1024]{1,0:T(8,128)}, f32[128,1024]{1,0:T(8,128)}) async-done(((f32[128,1024]{1,0:T(8,128)}, f32[128,1024]{1,0:T(8,128)}), (f32[128,1024]{1,0:T(8,128)}, f32[128,1024]{1,0:T(8,128)})) %all-reduce.3.cloned.1.call-update) | async-done | bytes 1048592 | tf_op jit(solution)/shard_map/psum | solution.py:63
  100.6 2.4 %fusion.6 = bf16[128,1024]{1,0:T(8,128)(2,1)S(1)} fusion(bf16[1,1024,1024]{2,1,0:T(8,128)(2,1)} %param.14, f32[128,1024]{1,0:T(8,128)} %get-tuple-element.5, f32[128,1024]{1,0:T(8,128)} %get-tuple-element.6), kind=kOutput, calls=%fused_computation.7 | convolution fusion | flops 269352960 | bytes 3407872 | tf_op jit(solution)/shard_map/dot_general | solution.py:65
  103.0 0.7 fusion.39
  103.7 5.5 %all-to-all-start.4 = ((bf16[8,16,256]{2,1,0:T(8,128)(2,1)}), bf16[8,16,256]{2,1,0:T(8,128)(2,1)S(1)}, u32[]{:S(2)}, u32[]{:S(2)}) async-start(bf16[8,16,256]{2,1,0:T(8,128)(2,1)} %bitcast.11), calls=%async_computation.4 | async-start | bytes 131072 | tf_op jit(solution)/shard_map/all_to_all | solution.py:71
  109.2 0.1 select_reduce_fusion
  109.3 6.8 %all-to-all-done.4 = bf16[8,16,256]{2,1,0:T(8,128)(2,1)S(1)} async-done(((bf16[8,16,256]{2,1,0:T(8,128)(2,1)}), bf16[8,16,256]{2,1,0:T(8,128)(2,1)S(1)}, u32[]{:S(2)}, u32[]{:S(2)}) %all-to-all-start.4) | async-done | bytes 65568 | tf_op jit(solution)/shard_map/all_to_all | solution.py:71
  116.1 3.3 %all-to-all-start.5 = ((bf16[8,16,256]{2,1,0:T(8,128)(2,1)}), bf16[8,16,256]{2,1,0:T(8,128)(2,1)S(1)}, u32[]{:S(2)}, u32[]{:S(2)}) async-start(bf16[8,16,256]{2,1,0:T(8,128)(2,1)} %bitcast.13), calls=%async_computation.5 | async-start | bytes 131072 | tf_op jit(solution)/shard_map/all_to_all | solution.py:71
  119.5 0.1 convolution_convert_fusion.7
  119.6 6.7 %all-to-all-done.5 = bf16[8,16,256]{2,1,0:T(8,128)(2,1)S(1)} async-done(((bf16[8,16,256]{2,1,0:T(8,128)(2,1)}), bf16[8,16,256]{2,1,0:T(8,128)(2,1)S(1)}, u32[]{:S(2)}, u32[]{:S(2)}) %all-to-all-start.5) | async-done | bytes 65568 | tf_op jit(solution)/shard_map/all_to_all | solution.py:71
  126.3 3.3 %all-to-all-start.6 = ((bf16[8,16,256]{2,1,0:T(8,128)(2,1)}), bf16[8,16,256]{2,1,0:T(8,128)(2,1)S(1)}, u32[]{:S(2)}, u32[]{:S(2)}) async-start(bf16[8,16,256]{2,1,0:T(8,128)(2,1)} %bitcast.15), calls=%async_computation.6 | async-start | bytes 131072 | tf_op jit(solution)/shard_map/all_to_all | solution.py:71
  129.7 0.1 convolution_convert_fusion.6
  129.8 6.7 %all-to-all-done.6 = bf16[8,16,256]{2,1,0:T(8,128)(2,1)S(1)} async-done(((bf16[8,16,256]{2,1,0:T(8,128)(2,1)}), bf16[8,16,256]{2,1,0:T(8,128)(2,1)S(1)}, u32[]{:S(2)}, u32[]{:S(2)}) %all-to-all-start.6) | async-done | bytes 65568 | tf_op jit(solution)/shard_map/all_to_all | solution.py:71
  136.5 3.3 %all-to-all-start.7 = ((bf16[8,16,256]{2,1,0:T(8,128)(2,1)}), bf16[8,16,256]{2,1,0:T(8,128)(2,1)S(1)}, u32[]{:S(2)}, u32[]{:S(2)}) async-start(bf16[8,16,256]{2,1,0:T(8,128)(2,1)} %bitcast.17), calls=%async_computation.7 | async-start | bytes 131072 | tf_op jit(solution)/shard_map/all_to_all | solution.py:71
  139.9 0.1 convolution_convert_fusion.5
  140.0 6.7 %all-to-all-done.7 = bf16[8,16,256]{2,1,0:T(8,128)(2,1)S(1)} async-done(((bf16[8,16,256]{2,1,0:T(8,128)(2,1)}), bf16[8,16,256]{2,1,0:T(8,128)(2,1)S(1)}, u32[]{:S(2)}, u32[]{:S(2)}) %all-to-all-start.7) | async-done | bytes 65568 | tf_op jit(solution)/shard_map/all_to_all | solution.py:71
  146.7 0.1 convolution_convert_fusion.4
  146.9 0.7 pad_maximum_fusion.3
  (14 shorter events, 0.0 us)
Async XLA Ops:
  6.5 57.6 %copy-start = (bf16[1,1024,1024]{2,1,0:T(8,128)(2,1)S(1)}, bf16[1,1024,1024]{2,1,0:T(8,128)(2,1)}, u32[]{:S(2)}) copy-start(bf16[1,1024,1024]{2,1,0:T(8,128)(2,1)} %param.12) | copy-start | bytes 6291460
  6.5 5.2 %copy-start.2 = (f32[2,2]{1,0:T(2,128)S(1)}, f32[2,2]{1,0:T(2,128)}, u32[]{:S(2)}) copy-start(f32[2,2]{1,0:T(2,128)} %constant.30.clone) | copy-start | bytes 52
  14.1 4.0 %copy-start.5 = (s32[1024]{0:T(1024)S(1)}, s32[1024]{0:T(1024)}, u32[]{:S(2)}) copy-start(s32[1024]{0:T(1024)} %param.9) | copy-start | bytes 12292
  14.1 4.1 %copy-start.3 = (bf16[16,1024]{1,0:T(8,128)(2,1)S(1)}, bf16[16,1024]{1,0:T(8,128)(2,1)}, u32[]{:S(2)}) copy-start(bf16[16,1024]{1,0:T(8,128)(2,1)} %param.8) | copy-start | bytes 98308
  14.1 4.4 %copy-start.4 = (s32[16,4]{0,1:T(4,128)S(1)}, s32[16,4]{0,1:T(4,128)}, u32[]{:S(2)}) copy-start(s32[16,4]{0,1:T(4,128)} %param.10) | copy-start | bytes 772
  20.2 14.2 %all-to-all-start = ((bf16[8,16,256]{2,1,0:T(8,128)(2,1)}), bf16[8,16,256]{2,1,0:T(8,128)(2,1)S(1)}, u32[]{:S(2)}, u32[]{:S(2)}) async-start(bf16[8,16,256]{2,1,0:T(8,128)(2,1)} %bitcast), calls=%async_computation | async-start | bytes 131072 | tf_op jit(solution)/shard_map/all_to_all | solution.py:59
  34.3 10.2 %all-to-all-start.1 = ((bf16[8,16,256]{2,1,0:T(8,128)(2,1)}), bf16[8,16,256]{2,1,0:T(8,128)(2,1)S(1)}, u32[]{:S(2)}, u32[]{:S(2)}) async-start(bf16[8,16,256]{2,1,0:T(8,128)(2,1)} %bitcast.2), calls=%async_computation.1 | async-start | bytes 131072 | tf_op jit(solution)/shard_map/all_to_all | solution.py:59
  44.5 10.2 %all-to-all-start.2 = ((bf16[8,16,256]{2,1,0:T(8,128)(2,1)}), bf16[8,16,256]{2,1,0:T(8,128)(2,1)S(1)}, u32[]{:S(2)}, u32[]{:S(2)}) async-start(bf16[8,16,256]{2,1,0:T(8,128)(2,1)} %bitcast.4), calls=%async_computation.2 | async-start | bytes 131072 | tf_op jit(solution)/shard_map/all_to_all | solution.py:59
  47.9 52.7 %all-reduce.3.cloned.1.call-start = ((), (), s32[]{:S(2)}) async-start(), calls=%async_computation.8 | async-start | bytes 2097152 | tf_op jit(solution)/shard_map/psum | solution.py:63
  54.7 10.7 %copy-start.1 = (bf16[1,1024,1024]{2,1,0:T(8,128)(2,1)S(1)}, bf16[1,1024,1024]{2,1,0:T(8,128)(2,1)}, u32[]{:S(2)}) copy-start(bf16[1,1024,1024]{2,1,0:T(8,128)(2,1)} %param.13) | copy-start | bytes 6291460
  100.6 8.7 %copy-start.6 = (f32[16,4]{0,1:T(4,128)S(1)}, f32[16,4]{0,1:T(4,128)}, u32[]{:S(2)}) copy-start(f32[16,4]{0,1:T(4,128)} %param.11) | copy-start | bytes 772
  103.7 12.4 %all-to-all-start.4 = ((bf16[8,16,256]{2,1,0:T(8,128)(2,1)}), bf16[8,16,256]{2,1,0:T(8,128)(2,1)S(1)}, u32[]{:S(2)}, u32[]{:S(2)}) async-start(bf16[8,16,256]{2,1,0:T(8,128)(2,1)} %bitcast.11), calls=%async_computation.4 | async-start | bytes 131072 | tf_op jit(solution)/shard_map/all_to_all | solution.py:71
  116.1 10.2 %all-to-all-start.5 = ((bf16[8,16,256]{2,1,0:T(8,128)(2,1)}), bf16[8,16,256]{2,1,0:T(8,128)(2,1)S(1)}, u32[]{:S(2)}, u32[]{:S(2)}) async-start(bf16[8,16,256]{2,1,0:T(8,128)(2,1)} %bitcast.13), calls=%async_computation.5 | async-start | bytes 131072 | tf_op jit(solution)/shard_map/all_to_all | solution.py:71
  126.3 10.2 %all-to-all-start.6 = ((bf16[8,16,256]{2,1,0:T(8,128)(2,1)}), bf16[8,16,256]{2,1,0:T(8,128)(2,1)S(1)}, u32[]{:S(2)}, u32[]{:S(2)}) async-start(bf16[8,16,256]{2,1,0:T(8,128)(2,1)} %bitcast.15), calls=%async_computation.6 | async-start | bytes 131072 | tf_op jit(solution)/shard_map/all_to_all | solution.py:71
  136.5 10.2 %all-to-all-start.7 = ((bf16[8,16,256]{2,1,0:T(8,128)(2,1)}), bf16[8,16,256]{2,1,0:T(8,128)(2,1)S(1)}, u32[]{:S(2)}, u32[]{:S(2)}) async-start(bf16[8,16,256]{2,1,0:T(8,128)(2,1)} %bitcast.17), calls=%async_computation.7 | async-start | bytes 131072 | tf_op jit(solution)/shard_map/all_to_all | solution.py:71
Sparse Core Ops, SparseCore 0:
  66.8 33.7 all-reduce.2
where the time goes:
time: 155 us; the launch traced here: 154 us
  waiting for transfers between devices  78.4 us (51%)
  starting transfers between devices  29.6 us (19%)
  between operations  13.6 us (9%)
  matrix products  9.55 us (6%)
  blocking collectives  9.41 us (6%)
  other arithmetic  7.66 us (5%)
  local copies, waits for them, and re-layouts  6.16 us (4%)
    psum x1, waiting for transfers between devices, per_device(): gate_full, up_full = lax.psum((gate_part, up_part), 'local')  33.9 us
    all_to_all x4, waiting for transfers between devices, per_device(): lax.all_to_all(out_block, 'node', split_axis=0, concat_axis=0, tiled=True)  27 us
    all_to_all x3, waiting for transfers between devices, per_device(): lax.all_to_all(outgoing, 'node', split_axis=0, concat_axis=0, tiled=True)  17.6 us
    all_to_all x4, starting transfers between devices, per_device(): lax.all_to_all(out_block, 'node', split_axis=0, concat_axis=0, tiled=True)  15.6 us
    all_to_all x3, starting transfers between devices, per_device(): lax.all_to_all(outgoing, 'node', split_axis=0, concat_axis=0, tiled=True)  14 us
    all_to_all x1, blocking collectives, per_device(): lax.all_to_all(outgoing, 'node', split_axis=0, concat_axis=0, tiled=True)  9.41 us
    mul x5, other arithmetic, hadamard_table(): matrix = jnp.kron(matrix, kernel_two)  4.11 us
    div x1, local copies, waits for them, and re-layouts, hadamard_table(): return matrix / math.sqrt(block_order)  4.02 us
  transfers between devices with their start and end apart: 8, of which 8 were waited for; matrix products, arithmetic and copies ran while one was open for 2% of the time, Pallas kernels for 0%

commit v1 on v0

--- a/solution.py
+++ b/solution.py
@@ -1,11 +1,269 @@
+import functools
 import math
 
 import jax
 import jax.numpy as jnp
 from jax import lax
+from jax.experimental import pallas as pl
+from jax.experimental.pallas import tpu as pltpu
 from jax.sharding import PartitionSpec as P
 
 HB = 128
+LANES = 128
+CHUNKS = 4
+MESH = pl.DeviceIdType.MESH
+
+
+def fused_kernel(
+    nodes,
+    tok_ref, sign_ref, routes_ref, gv_ref, gw_hbm, uw_hbm, dw_hbm, out_ref,
+    gw, uw, dw, arr, core_out, core_in, y_out, y_in, hid, acc, wf, x_out, x_in, z_own, z_out, z_in,
+    w_sem, ag_send, ag_recv, fw_send, core_send, core_recv, y_send, y_recv,
+    hid_send, hid_recv, x_send, x_recv, z_send, z_recv,
+):
+    rows, width = tok_ref.shape
+    nz = nodes // 2
+    total = nodes * rows
+    half = total // 2
+    piece = gw.shape[1] // 4
+    cols = width // CHUNKS
+    f32, bf16 = jnp.float32, jnp.bfloat16
+
+    node = lax.axis_index("node")
+    local = lax.axis_index("local")
+    z, x = node // 2, node % 2
+    y, c = local // 2, local % 2
+    x_peer = {"node": z * 2 + (1 - x)}
+    z_peers = [(z + step) % nz for step in range(1, nz)]
+    core_peer_l = y * 2 + (1 - c)
+    y_peer_l = (1 - y) * 2 + c
+    core_peer = {"local": core_peer_l}
+    y_peer = {"local": y_peer_l}
+
+    loads = []
+    for i, (src, dst) in enumerate(((gw_hbm, gw), (uw_hbm, uw), (dw_hbm, dw))):
+        load = pltpu.make_async_copy(src.at[0], dst, w_sem.at[i])
+        load.start()
+        loads.append(load)
+
+    barrier = pltpu.get_barrier_semaphore()
+    peers = [x_peer, core_peer, y_peer] + [{"node": pz * 2 + x} for pz in z_peers]
+    for peer in peers:
+        pl.semaphore_signal(barrier, inc=1, device_id=peer, device_id_type=MESH)
+
+    row_id = lax.broadcasted_iota(jnp.int32, (HB, HB), 0)
+    col_id = lax.broadcasted_iota(jnp.int32, (HB, HB), 1)
+    bits = row_id & col_id
+    bits = bits ^ (bits >> 4)
+    bits = bits ^ (bits >> 2)
+    bits = bits ^ (bits >> 1)
+    table = (1 - 2 * (bits & 1)).astype(f32).astype(bf16)
+    me = x * nz + z
+    signs = (1 - 2 * sign_ref[...]).astype(f32)
+    signed = (tok_ref[...].astype(f32) * signs).astype(bf16)
+    for b in range(width // HB):
+        block = jnp.dot(signed[:, b * HB : (b + 1) * HB], table, preferred_element_type=f32)
+        arr[me, :, b * HB : (b + 1) * HB] = (block * (1.0 / math.sqrt(HB))).astype(bf16)
+    lane = lax.broadcasted_iota(jnp.int32, (rows, LANES), 1)
+    dense = jnp.zeros((rows, LANES), f32)
+    for k in range(routes_ref.shape[1]):
+        hit = (lane % nodes) == routes_ref[:, k : k + 1]
+        dense = dense + jnp.where(hit, gv_ref[:, k : k + 1], 0.0)
+    high = dense.astype(bf16).astype(f32)
+    middle = (dense - high).astype(bf16).astype(f32)
+    low = dense - high - middle
+    parts = jnp.where(lane < nodes, high, jnp.where(lane < 2 * nodes, middle, low))
+    parts = jnp.where(lane < 3 * nodes, parts, 0.0)
+    arr[me, :, width:] = parts.astype(bf16)
+
+    pl.semaphore_wait(barrier, len(peers))
+
+    def gather(slot, send_sem, peer):
+        return pltpu.make_async_remote_copy(
+            src_ref=arr.at[slot], dst_ref=arr.at[slot], send_sem=send_sem,
+            recv_sem=ag_recv.at[slot], device_id=peer, device_id_type=MESH,
+        )
+
+    sent = []
+    for i, pz in enumerate(z_peers):
+        copy = gather(me, ag_send.at[i], {"node": pz * 2 + x})
+        copy.start()
+        sent.append(copy)
+    copy = gather(me, fw_send.at[nz - 1], x_peer)
+    copy.start()
+    sent.append(copy)
+    for i, pz in enumerate(z_peers):
+        copy = gather(x * nz + pz, fw_send.at[i], x_peer)
+        copy.wait_recv()
+        copy.start()
+        sent.append(copy)
+    for pz in [z] + z_peers:
+        gather((1 - x) * nz + pz, fw_send.at[0], x_peer).wait_recv()
+
+    loads[0].wait()
+    loads[1].wait()
+
+    def partial_sums(p):
+        where = pl.ds(pl.multiple_of(p * piece, piece), piece)
+        tokens = arr[:, :, :width].reshape(total, width)
+        gate = jnp.dot(tokens, gw[:, where], preferred_element_type=f32)
+        up = jnp.dot(tokens, uw[:, where], preferred_element_type=f32)
+        return gate, up
+
+    def push(src, dst, send_sem, recv_sem, peer):
+        copy = pltpu.make_async_remote_copy(
+            src_ref=src, dst_ref=dst, send_sem=send_sem, recv_sem=recv_sem,
+            device_id=peer, device_id_type=MESH,
+        )
+        copy.start()
+        sent.append(copy)
+        return copy
+
+    def to_core(i, p):
+        gate, up = partial_sums(p)
+        core_out[i, :, :piece] = gate.astype(bf16)
+        core_out[i, :, piece:] = up.astype(bf16)
+        return push(core_out.at[i], core_in.at[i], core_send.at[i], core_recv.at[i], core_peer)
+
+    first = to_core(0, (1 - y) * 2 + (1 - c))
+    gate, up = partial_sums((1 - y) * 2 + c)
+    first.wait_recv()
+    y_out[:, :piece] = (gate + core_in[0, :, :piece].astype(f32)).astype(bf16)
+    y_out[:, piece:] = (up + core_in[0, :, piece:].astype(f32)).astype(bf16)
+    over_y = push(y_out, y_in, y_send.at[0], y_recv.at[0], y_peer)
+    second = to_core(1, y * 2 + (1 - c))
+    gate, up = partial_sums(local)
+    second.wait_recv()
+    gate = gate + core_in[1, :, :piece].astype(f32)
+    up = up + core_in[1, :, piece:].astype(f32)
+    over_y.wait_recv()
+    gate = gate + y_in[:, :piece].astype(f32)
+    up = up + y_in[:, piece:].astype(f32)
+    hid[local] = (gate / (1.0 + jnp.exp(-gate)) * up).astype(bf16)
+
+    def spread(p, i, peer):
+        return pltpu.make_async_remote_copy(
+            src_ref=hid.at[p], dst_ref=hid.at[p], send_sem=hid_send.at[i],
+            recv_sem=hid_recv.at[p], device_id=peer, device_id_type=MESH,
+        )
+
+    for i, peer in enumerate((y_peer, core_peer)):
+        copy = spread(local, i, peer)
+        copy.start()
+        sent.append(copy)
+    loads[2].wait()
+
+    def down(p, where):
+        depth = pl.ds(pl.multiple_of(p * piece, piece), piece)
+        return jnp.dot(hid[p], dw[depth, where], preferred_element_type=f32)
+
+    chunk_at = [slice(j * cols, (j + 1) * cols) for j in range(CHUNKS)]
+    for where in chunk_at:
+        acc[:, where] = down(local, where)
+    spread(core_peer_l, 0, core_peer).wait_recv()
+    for where in chunk_at:
+        acc[:, where] += down(core_peer_l, where)
+    copy = spread(y_peer_l, 2, core_peer)
+    copy.wait_recv()
+    copy.start()
+    sent.append(copy)
+    for where in chunk_at:
+        acc[:, where] += down(y_peer_l, where)
+    last_l = (1 - y) * 2 + (1 - c)
+    spread(last_l, 0, core_peer).wait_recv()
+
+    lane = lax.broadcasted_iota(jnp.int32, (total, LANES), 1)
+    mine = (lane == node) | (lane == node + nodes) | (lane == node + 2 * nodes)
+    coded = arr[:, :, width:].reshape(total, LANES).astype(f32)
+    weight = jnp.sum(jnp.where(mine, coded, 0.0), axis=1, keepdims=True)
+
+    over_x = []
+    for j, where in enumerate(chunk_at):
+        result = (acc[:, where] + down(last_l, where)).astype(bf16).astype(f32)
+        weighted = (result * weight).reshape(2, half, cols)
+        wf[j] = weighted
+        x_out[j] = weighted.astype(bf16)
+        over_x.append(push(x_out.at[j, 1 - x], x_in.at[j], x_send.at[j], x_recv.at[j], x_peer))
+    for j, where in enumerate(chunk_at):
+        over_x[j].wait_recv()
+        summed = (wf[j, x] + x_in[j].astype(f32)).reshape(nz, rows, cols)
+        z_own[j] = summed
+        z_out[j] = summed.astype(bf16)
+        for i, pz in enumerate(z_peers):
+            push(z_out.at[j, pz], z_in.at[j, i], z_send.at[j, i], z_recv.at[j, i], {"node": pz * 2 + x})
+    for j, where in enumerate(chunk_at):
+        mixed = z_own[j, z]
+        for i in range(nz - 1):
+            pltpu.make_async_remote_copy(
+                src_ref=z_out.at[j, z], dst_ref=z_in.at[j, i], send_sem=z_send.at[j, i],
+                recv_sem=z_recv.at[j, i], device_id=x_peer, device_id_type=MESH,
+            ).wait_recv()
+            mixed = mixed + z_in[j, i].astype(f32)
+        out_ref[:, where] = mixed.astype(bf16)
+
+    for copy in sent:
+        copy.wait_send()
+
+
+def fused(tokens, sign_bits, routes, gate_values, gate_w, up_w, down_w):
+    nodes = lax.axis_size("node")
+    rows, width = tokens.shape
+    hidden = gate_w.shape[2]
+    total, nz, piece, cols = nodes * rows, nodes // 2, hidden // 4, width // CHUNKS
+    bf16, f32 = jnp.bfloat16, jnp.float32
+    dma = pltpu.SemaphoreType.DMA
+    vmem = pl.BlockSpec(memory_space=pltpu.VMEM)
+    hbm = pl.BlockSpec(memory_space=pl.ANY)
+    return pl.pallas_call(
+        functools.partial(fused_kernel, nodes),
+        out_shape=jax.ShapeDtypeStruct((rows, width), bf16),
+        in_specs=[vmem] * 4 + [hbm] * 3,
+        out_specs=vmem,
+        scratch_shapes=[
+            pltpu.VMEM((width, hidden), bf16),
+            pltpu.VMEM((width, hidden), bf16),
+            pltpu.VMEM((hidden, width), bf16),
+            pltpu.VMEM((nodes, rows, width + LANES), bf16),
+            pltpu.VMEM((2, total, 2 * piece), bf16),
+            pltpu.VMEM((2, total, 2 * piece), bf16),
+            pltpu.VMEM((total, 2 * piece), bf16),
+            pltpu.VMEM((total, 2 * piece), bf16),
+            pltpu.VMEM((4, total, piece), bf16),
+            pltpu.VMEM((total, width), f32),
+            pltpu.VMEM((CHUNKS, 2, total // 2, cols), f32),
+            pltpu.VMEM((CHUNKS, 2, total // 2, cols), bf16),
+            pltpu.VMEM((CHUNKS, total // 2, cols), bf16),
+            pltpu.VMEM((CHUNKS, nz, rows, cols), f32),
+            pltpu.VMEM((CHUNKS, nz, rows, cols), bf16),
+            pltpu.VMEM((CHUNKS, nz - 1, rows, cols), bf16),
+            dma((3,)),
+            dma((nz - 1,)), dma((nodes,)), dma((nz,)),
+            dma((2,)), dma((2,)), dma((1,)), dma((1,)),
+            dma((3,)), dma((4,)),
+            dma((CHUNKS,)), dma((CHUNKS,)),
+            dma((CHUNKS, nz - 1)), dma((CHUNKS, nz - 1)),
+        ],
+        compiler_params=pltpu.CompilerParams(
+            collective_id=0, has_side_effects=True, vmem_limit_bytes=48 * 1024 * 1024
+        ),
+        cost_estimate=pl.CostEstimate(
+            flops=6 * total * width * hidden, bytes_accessed=6 * width * hidden, transcendentals=0
+        ),
+    )(tokens, sign_bits.reshape(1, width), routes, gate_values, gate_w, up_w, down_w)
+
+
+def fits_fused(tokens, routes, gate_w, capacity):
+    nodes, rows = lax.axis_size("node"), tokens.shape[0]
+    return (
+        capacity >= rows
+        and nodes % 2 == 0
+        and 4 <= nodes <= 16
+        and lax.axis_size("local") == 4
+        and rows % 16 == 0
+        and nodes * rows <= 256
+        and tokens.shape[1] % (CHUNKS * LANES) == 0
+        and gate_w.shape[2] % (4 * LANES) == 0
+    )
 
 
 def hadamard_table(block_order):
@@ -32,6 +290,8 @@
     tok_node, width_dev = tokens.shape
     top_count = routes.shape[1]
     capacity = max(2, 2 * tok_node * top_count // experts)
+    if fits_fused(tokens, routes, gate_w, capacity):
+        return fused(tokens, sign_bits, routes, gate_values, gate_w, up_w, down_w)
     placed = slot_table(routes, experts, capacity).reshape(experts * capacity, tok_node, top_count)
     scatter_mat = jnp.any(placed, axis=2).astype(jnp.bfloat16)
     combine_mat = jnp.sum(placed.astype(jnp.float32) * gate_values[None, :, :], axis=2)

time: 155 us -> 40.3 us (0.26)
  waiting for transfers between devices: 78.4 us -> 0 us
  Pallas kernels: 0 us -> 33.2 us
  starting transfers between devices: 29.6 us -> 0 us
  between operations: 13.6 us -> 0.01 us
  matrix products: 9.55 us -> 0 us
  blocking collectives: 9.41 us -> 0 us
  other arithmetic: 7.66 us -> 0 us
    all_to_all x7 -> x0, waiting for transfers between devices: 44.6 us -> none  [the longest x4 27 us: per_device(): lax.all_to_all(out_block, 'node', split_axis=0, concat_axis=0, tiled=True)]
    psum x1 -> x0, waiting for transfers between devices: 33.9 us -> none  [per_device(): gate_full, up_full = lax.psum((gate_part, up_part), 'local')]
    pallas_call x0 -> x1, Pallas kernels: none -> 33.2 us  [fused(): pl.pallas_call(functools.partial(fused_kernel, nodes), out_shape=jax.Shap...]
    all_to_all x7 -> x0, starting transfers between devices: 29.5 us -> none  [the longest x4 15.6 us: per_device(): lax.all_to_all(out_block, 'node', split_axis=0, concat_axis=0, tiled=True)]
    dot_general x19 -> x0, matrix products: 9.55 us -> none  [the longest x4 2.77 us: per_device(): jnp.dot(scatter_mat, rotated, preferred_element_type=jnp.float32)]
    all_to_all x1 -> x0, blocking collectives: 9.41 us -> none  [per_device(): lax.all_to_all(outgoing, 'node', split_axis=0, concat_axis=0, tiled=True)]
    unnamed x15 -> x11, local copies, waits for them, and re-layouts: 0.11 us -> 6.76 us
    mul x6 -> x0, other arithmetic: 4.12 us -> none  [the longest x5 4.11 us: hadamard_table(): matrix = jnp.kron(matrix, kernel_two)]
  transfers between devices with their start and end apart: 8 -> 0, of which waited for: 8 -> 0; matrix products, arithmetic and copies ran while one was open for 2% -> 0% of each run, Pallas kernels for 0% -> 0%
where the time goes in v1:
time: 40.3 us; the launch traced here: 40 us
  Pallas kernels  33.2 us (82%)
  local copies, waits for them, and re-layouts  6.76 us (17%)
    pallas_call x1, Pallas kernels, fused(): pl.pallas_call(functools.partial(fused_kernel, nodes), out_shape=jax.Shap...  33.2 us
    unnamed x11, local copies, waits for them, and re-layouts  6.76 us

profile of v1, /device:TPU:0, one launch (start us, length us, event | category | flops | bytes accessed | tf_op | source)
XLA Modules:
  0.0 40.0 jit_solution(8977730680125287523)
XLA Ops:
  0.0 0.8 %copy.8.routes_ref = s32[16,4]{1,0:T(8,128)S(1)} copy(s32[16,4]{0,1:T(4,128)} %param.9) | data formatting | bytes 512 | tf_op args[2]
  0.8 0.8 %copy.9.gv_ref = f32[16,4]{1,0:T(8,128)S(1)} copy(f32[16,4]{0,1:T(4,128)} %param.10) | data formatting | bytes 512 | tf_op args[3]
  1.5 0.0 copy-start
  1.5 1.6 %copy-done = bf16[1,1024,1024]{2,1,0:T(8,128)(2,1)S(1)} copy-done((bf16[1,1024,1024]{2,1,0:T(8,128)(2,1)S(1)}, bf16[1,1024,1024]{2,1,0:T(8,128)(2,1)}, u32[]{:S(2)}) %copy-start) | copy-done | bytes 2097176
  3.1 0.0 copy-start.1
  3.1 1.6 %copy-done.1 = bf16[1,1024,1024]{2,1,0:T(8,128)(2,1)S(1)} copy-done((bf16[1,1024,1024]{2,1,0:T(8,128)(2,1)S(1)}, bf16[1,1024,1024]{2,1,0:T(8,128)(2,1)}, u32[]{:S(2)}) %copy-start.1) | copy-done | bytes 2097176
  4.7 0.0 copy-start.2
  4.7 0.8 %copy-done.2 = bf16[16,1024]{1,0:T(8,128)(2,1)S(1)} copy-done((bf16[16,1024]{1,0:T(8,128)(2,1)S(1)}, bf16[16,1024]{1,0:T(8,128)(2,1)}, u32[]{:S(2)}) %copy-start.2) | copy-done | bytes 32792
  5.5 0.0 copy-start.3
  5.5 0.7 %copy-done.3 = s32[1024]{0:T(1024)S(1)} copy-done((s32[1024]{0:T(1024)S(1)}, s32[1024]{0:T(1024)}, u32[]{:S(2)}) %copy-start.3) | copy-done | bytes 4120
  6.1 33.2 %shard_map.73 = bf16[16,1024]{1,0:T(8,128)(2,1)S(1)} custom-call(bf16[16,1024]{1,0:T(8,128)(2,1)S(1)} %copy-done.2, s32[1,1024]{1,0:T(1,128)S(1)} %bitcast.1, s32[16,4]{1,0:T(8,128)S(1)} %copy.8.routes_ref, f32[16,4]{1,0:T(8,128)S(1)} %copy.9.gv_ref, bf16[1,1024,1024]{2,1,0:T(8,128)(2,1)S(1)} %copy-done, bf16[1,1024,1024]{2,1,0:T(8,128)(2,1)S(1)} %copy-done.1, ...), custom_call_target="tpu_custom_call" | custom-call | flops 805306368 | bytes 6291456 | tf_op jit(solution)/shard_map/pallas_call | solution.py:217
  39.4 0.6 %copy.11 = bf16[16,1024]{1,0:T(8,128)(2,1)} copy(bf16[16,1024]{1,0:T(8,128)(2,1)S(1)} %shard_map.73) | data formatting | bytes 65536
Async XLA Ops:
  1.5 1.6 %copy-start = (bf16[1,1024,1024]{2,1,0:T(8,128)(2,1)S(1)}, bf16[1,1024,1024]{2,1,0:T(8,128)(2,1)}, u32[]{:S(2)}) copy-start(bf16[1,1024,1024]{2,1,0:T(8,128)(2,1)} %gw_hbm.1) | copy-start | bytes 6291460
  3.1 1.6 %copy-start.1 = (bf16[1,1024,1024]{2,1,0:T(8,128)(2,1)S(1)}, bf16[1,1024,1024]{2,1,0:T(8,128)(2,1)}, u32[]{:S(2)}) copy-start(bf16[1,1024,1024]{2,1,0:T(8,128)(2,1)} %uw_hbm.1) | copy-start | bytes 6291460
  4.7 0.8 %copy-start.2 = (bf16[16,1024]{1,0:T(8,128)(2,1)S(1)}, bf16[16,1024]{1,0:T(8,128)(2,1)}, u32[]{:S(2)}) copy-start(bf16[16,1024]{1,0:T(8,128)(2,1)} %tok_ref.1) | copy-start | bytes 98308
  5.5 0.7 %copy-start.3 = (s32[1024]{0:T(1024)S(1)}, s32[1024]{0:T(1024)}, u32[]{:S(2)}) copy-start(s32[1024]{0:T(1024)} %param.8) | copy-start | bytes 12292

commit v2 on v1

--- a/solution.py
+++ b/solution.py
@@ -11,17 +11,18 @@
 HB = 128
 LANES = 128
 CHUNKS = 4
+VMEM_BYTES = 64 * 1024 * 1024
 MESH = pl.DeviceIdType.MESH
 
 
 def fused_kernel(
     nodes,
-    tok_ref, sign_ref, routes_ref, gv_ref, gw_hbm, uw_hbm, dw_hbm, out_ref,
-    gw, uw, dw, arr, core_out, core_in, y_out, y_in, hid, acc, wf, x_out, x_in, z_own, z_out, z_in,
+    tok_hbm, sign_hbm, routes_hbm, gv_hbm, gw_hbm, uw_hbm, dw_hbm, out_ref,
+    tok_ref, sign_ref, routes_ref, gv_ref, gw, uw, dw, arr, core_out, core_in, y_out, y_in, hid, acc, wf, x_out, x_in, z_own, z_out, z_in,
     w_sem, ag_send, ag_recv, fw_send, core_send, core_recv, y_send, y_recv,
     hid_send, hid_recv, x_send, x_recv, z_send, z_recv,
 ):
-    rows, width = tok_ref.shape
+    rows, width = tok_hbm.shape
     nz = nodes // 2
     total = nodes * rows
     half = total // 2
@@ -40,16 +41,19 @@
     core_peer = {"local": core_peer_l}
     y_peer = {"local": y_peer_l}
 
-    loads = []
-    for i, (src, dst) in enumerate(((gw_hbm, gw), (uw_hbm, uw), (dw_hbm, dw))):
-        load = pltpu.make_async_copy(src.at[0], dst, w_sem.at[i])
-        load.start()
-        loads.append(load)
-
     barrier = pltpu.get_barrier_semaphore()
     peers = [x_peer, core_peer, y_peer] + [{"node": pz * 2 + x} for pz in z_peers]
     for peer in peers:
         pl.semaphore_signal(barrier, inc=1, device_id=peer, device_id_type=MESH)
+
+    loads = []
+    for i, (src, dst) in enumerate((
+        (tok_hbm, tok_ref), (sign_hbm, sign_ref), (routes_hbm, routes_ref), (gv_hbm, gv_ref),
+        (gw_hbm.at[0], gw), (uw_hbm.at[0], uw), (dw_hbm.at[0], dw),
+    )):
+        load = pltpu.make_async_copy(src, dst, w_sem.at[i])
+        load.start()
+        loads.append(load)
 
     row_id = lax.broadcasted_iota(jnp.int32, (HB, HB), 0)
     col_id = lax.broadcasted_iota(jnp.int32, (HB, HB), 1)
@@ -59,22 +63,28 @@
     bits = bits ^ (bits >> 1)
     table = (1 - 2 * (bits & 1)).astype(f32).astype(bf16)
     me = x * nz + z
+    for load in loads[:4]:
+        load.wait()
     signs = (1 - 2 * sign_ref[...]).astype(f32)
     signed = (tok_ref[...].astype(f32) * signs).astype(bf16)
     for b in range(width // HB):
         block = jnp.dot(signed[:, b * HB : (b + 1) * HB], table, preferred_element_type=f32)
         arr[me, :, b * HB : (b + 1) * HB] = (block * (1.0 / math.sqrt(HB))).astype(bf16)
-    lane = lax.broadcasted_iota(jnp.int32, (rows, LANES), 1)
-    dense = jnp.zeros((rows, LANES), f32)
-    for k in range(routes_ref.shape[1]):
-        hit = (lane % nodes) == routes_ref[:, k : k + 1]
-        dense = dense + jnp.where(hit, gv_ref[:, k : k + 1], 0.0)
+    code = lax.broadcasted_iota(jnp.int32, (LANES, rows), 0)
+    dense = jnp.zeros((LANES, rows), f32)
+    for k in range(routes_ref.shape[0]):
+        hit = (code % nodes) == routes_ref[k : k + 1, :]
+        dense = dense + jnp.where(hit, gv_ref[k : k + 1, :], 0.0)
     high = dense.astype(bf16).astype(f32)
     middle = (dense - high).astype(bf16).astype(f32)
     low = dense - high - middle
-    parts = jnp.where(lane < nodes, high, jnp.where(lane < 2 * nodes, middle, low))
-    parts = jnp.where(lane < 3 * nodes, parts, 0.0)
-    arr[me, :, width:] = parts.astype(bf16)
+    parts = jnp.where(code < nodes, high, jnp.where(code < 2 * nodes, middle, low))
+    parts = jnp.where(code < 3 * nodes, parts, 0.0).astype(bf16)
+    same = lax.broadcasted_iota(jnp.int32, (rows, rows), 0) == lax.broadcasted_iota(jnp.int32, (rows, rows), 1)
+    turned = lax.dot_general(
+        same.astype(f32).astype(bf16), parts, (((1,), (1,)), ((), ())), preferred_element_type=f32
+    )
+    arr[me, :, width:] = turned.astype(bf16)
 
     pl.semaphore_wait(barrier, len(peers))
 
@@ -100,8 +110,8 @@
     for pz in [z] + z_peers:
         gather((1 - x) * nz + pz, fw_send.at[0], x_peer).wait_recv()
 
-    loads[0].wait()
-    loads[1].wait()
+    loads[4].wait()
+    loads[5].wait()
 
     def partial_sums(p):
         where = pl.ds(pl.multiple_of(p * piece, piece), piece)
@@ -151,7 +161,7 @@
         copy = spread(local, i, peer)
         copy.start()
         sent.append(copy)
-    loads[2].wait()
+    loads[6].wait()
 
     def down(p, where):
         depth = pl.ds(pl.multiple_of(p * piece, piece), piece)
@@ -217,9 +227,13 @@
     return pl.pallas_call(
         functools.partial(fused_kernel, nodes),
         out_shape=jax.ShapeDtypeStruct((rows, width), bf16),
-        in_specs=[vmem] * 4 + [hbm] * 3,
+        in_specs=[hbm] * 7,
         out_specs=vmem,
         scratch_shapes=[
+            pltpu.VMEM((rows, width), bf16),
+            pltpu.VMEM((1, width), jnp.int32),
+            pltpu.VMEM((routes.shape[1], rows), jnp.int32),
+            pltpu.VMEM((routes.shape[1], rows), f32),
             pltpu.VMEM((width, hidden), bf16),
             pltpu.VMEM((width, hidden), bf16),
             pltpu.VMEM((hidden, width), bf16),
@@ -236,7 +250,7 @@
             pltpu.VMEM((CHUNKS, nz, rows, cols), f32),
             pltpu.VMEM((CHUNKS, nz, rows, cols), bf16),
             pltpu.VMEM((CHUNKS, nz - 1, rows, cols), bf16),
-            dma((3,)),
+            dma((7,)),
             dma((nz - 1,)), dma((nodes,)), dma((nz,)),
             dma((2,)), dma((2,)), dma((1,)), dma((1,)),
             dma((3,)), dma((4,)),
@@ -244,12 +258,12 @@
             dma((CHUNKS, nz - 1)), dma((CHUNKS, nz - 1)),
         ],
         compiler_params=pltpu.CompilerParams(
-            collective_id=0, has_side_effects=True, vmem_limit_bytes=48 * 1024 * 1024
+            collective_id=0, has_side_effects=True, vmem_limit_bytes=VMEM_BYTES
         ),
         cost_estimate=pl.CostEstimate(
             flops=6 * total * width * hidden, bytes_accessed=6 * width * hidden, transcendentals=0
         ),
-    )(tokens, sign_bits.reshape(1, width), routes, gate_values, gate_w, up_w, down_w)
+    )(tokens, sign_bits.reshape(1, width), routes.T, gate_values.T, gate_w, up_w, down_w)
 
 
 def fits_fused(tokens, routes, gate_w, capacity):

time: 40.3 us -> 35.1 us (0.87)
  local copies, waits for them, and re-layouts: 6.76 us -> 1.38 us
    unnamed x11 -> x1, local copies, waits for them, and re-layouts: 6.76 us -> 1.38 us
where the time goes in v2:
time: 35.1 us; the launch traced here: 35 us
  Pallas kernels  33.6 us (96%)
  local copies, waits for them, and re-layouts  1.38 us (4%)
    pallas_call x1, Pallas kernels, fused(): pl.pallas_call(functools.partial(fused_kernel, nodes), out_shape=jax.Shap...  33.6 us
    unnamed x1, local copies, waits for them, and re-layouts  1.38 us

profile of v2, /device:TPU:0, one launch (start us, length us, event | category | flops | bytes accessed | tf_op | source)
XLA Modules:
  0.0 35.0 jit_solution(2064660415380409899)
XLA Ops:
  0.0 33.6 %shard_map.73 = bf16[16,1024]{1,0:T(8,128)(2,1)} custom-call(bf16[16,1024]{1,0:T(8,128)(2,1)} %tok_hbm.1, s32[1,1024]{1,0:T(1,128)} %bitcast.3, s32[4,16]{1,0:T(4,128)} %bitcast.4, f32[4,16]{1,0:T(4,128)} %bitcast.5, bf16[1,1024,1024]{2,1,0:T(8,128)(2,1)} %gw_hbm.1, bf16[1,1024,1024]{2,1,0:T(8,128)(2,1)} %uw_hbm.1, bf16[1,1024,1024]{2,1,0:T(8,128)(2,1)} %dw_hbm.1), custom_call_target="tpu_custom_call" | custom-call | flops 805306368 | bytes 6291456 | tf_op jit(solution)/shard_map/pallas_call | solution.py:227
  33.6 1.4 %copy.9 = bf16[16,1024]{1,0:T(8,128)(2,1)} copy(bf16[16,1024]{1,0:T(8,128)(2,1)} %shard_map.73) | data formatting | bytes 65536

commit v3 on v2

v3 whole, which is shorter than its diff:
```python
import functools
import math

import jax
import jax.numpy as jnp
from jax import lax
from jax.experimental import pallas as pl
from jax.experimental.pallas import tpu as pltpu
from jax.sharding import PartitionSpec as P

HB = 128
LANES = 128
CHUNKS = 2
VMEM_BYTES = 63 * 1024 * 1024
MESH = pl.DeviceIdType.MESH


def fused_kernel(
    nodes,
    tok_hbm, sign_hbm, routes_hbm, gv_hbm, gw_hbm, uw_hbm, dw_hbm, out_ref,
    tok_ref, sign_ref, routes_ref, gv_ref, gw, uw, dw, arr,
    core_out, core_in, y_out, y_in, hid, acc, own, back_out, back_in,
    w_sem, ag_send, ag_recv, fw_send, core_send, core_recv, y_send, y_recv,
    hid_send, hid_recv, back_send, back_recv,
):
    rows, width = tok_hbm.shape
    nz = nodes // 2
    half = nz * rows
    piece = gw.shape[1] // 4
    cols = width // CHUNKS
    f32, bf16 = jnp.float32, jnp.bfloat16

    node = lax.axis_index("node")
    local = lax.axis_index("local")
    z, x = node // 2, node % 2
    y, c = local // 2, local % 2
    x_peer = {"node": z * 2 + (1 - x)}
    z_peers = [(z + step) % nz for step in range(1, nz)]
    core_peer_l, y_peer_l, far_l = y * 2 + (1 - c), (1 - y) * 2 + c, (1 - y) * 2 + (1 - c)
    core_peer, y_peer, far_peer = {"local": core_peer_l}, {"local": y_peer_l}, {"local": far_l}
    same_plane = [{"node": pz * 2 + x} for pz in z_peers]
    other_plane = [{"node": pz * 2 + (1 - x)} for pz in [z] + z_peers]

    barrier = pltpu.get_barrier_semaphore()
    peers = [core_peer, y_peer, far_peer] + same_plane + other_plane
    for peer in peers:
        pl.semaphore_signal(barrier, inc=1, device_id=peer, device_id_type=MESH)

    loads = []
    for i, (src, dst) in enumerate((
        (tok_hbm, tok_ref), (sign_hbm, sign_ref), (routes_hbm, routes_ref), (gv_hbm, gv_ref),
        (gw_hbm.at[0], gw), (uw_hbm.at[0], uw), (dw_hbm.at[0], dw),
    )):
        load = pltpu.make_async_copy(src, dst, w_sem.at[i])
        load.start()
        loads.append(load)

    row_id = lax.broadcasted_iota(jnp.int32, (HB, HB), 0)
    col_id = lax.broadcasted_iota(jnp.int32, (HB, HB), 1)
    bits = row_id & col_id
    bits = bits ^ (bits >> 4)
    bits = bits ^ (bits >> 2)
    bits = bits ^ (bits >> 1)
    table = (1 - 2 * (bits & 1)).astype(f32).astype(bf16)
    for load in loads[:4]:
        load.wait()
    signs = (1 - 2 * sign_ref[...]).astype(f32)
    signed = (tok_ref[...].astype(f32) * signs).astype(bf16)
    for b in range(width // HB):
        block = jnp.dot(signed[:, b * HB : (b + 1) * HB], table, preferred_element_type=f32)
        arr[x, z, :, b * HB : (b + 1) * HB] = (block * (1.0 / math.sqrt(HB))).astype(bf16)
    code = lax.broadcasted_iota(jnp.int32, (LANES, rows), 0)
    dense = jnp.zeros((LANES, rows), f32)
    for k in range(routes_ref.shape[0]):
        hit = (code % nodes) == routes_ref[k : k + 1, :]
        dense = dense + jnp.where(hit, gv_ref[k : k + 1, :], 0.0)
    high = dense.astype(bf16).astype(f32)
    middle = (dense - high).astype(bf16).astype(f32)
    low = dense - high - middle
    parts = jnp.where(code < nodes, high, jnp.where(code < 2 * nodes, middle, low))
    parts = jnp.where(code < 3 * nodes, parts, 0.0).astype(bf16)
    same = lax.broadcasted_iota(jnp.int32, (rows, rows), 0) == lax.broadcasted_iota(jnp.int32, (rows, rows), 1)
    turned = lax.dot_general(
        same.astype(f32).astype(bf16), parts, (((1,), (1,)), ((), ())), preferred_element_type=f32
    )
    arr[x, z, :, width:] = turned.astype(bf16)

    pl.semaphore_wait(barrier, len(peers))

    def gather(plane, pz, send_sem, peer):
        return pltpu.make_async_remote_copy(
            src_ref=arr.at[plane, pz], dst_ref=arr.at[plane, pz], send_sem=send_sem,
            recv_sem=ag_recv.at[plane, pz], device_id=peer, device_id_type=MESH,
        )

    sent = []

    def start(copy):
        copy.start()
        sent.append(copy)
        return copy

    def push(src, dst, send_sem, recv_sem, peer):
        return start(pltpu.make_async_remote_copy(
            src_ref=src, dst_ref=dst, send_sem=send_sem, recv_sem=recv_sem,
            device_id=peer, device_id_type=MESH,
        ))

    for i, peer in enumerate(same_plane):
        start(gather(x, z, ag_send.at[i], peer))
    start(gather(x, z, fw_send.at[nz - 1], x_peer))
    for i, pz in enumerate(z_peers):
        copy = gather(x, pz, fw_send.at[i], x_peer)
        copy.wait_recv()
        start(copy)
    loads[4].wait()
    loads[5].wait()

    planes = (x, 1 - x)

    def partial_sums(group, p):
        where = pl.ds(pl.multiple_of(p * piece, piece), piece)
        tokens = arr[planes[group], :, :, :width].reshape(half, width)
        gate = jnp.dot(tokens, gw[:, where], preferred_element_type=f32)
        up = jnp.dot(tokens, uw[:, where], preferred_element_type=f32)
        return gate, up

    def to_core(i, group, p):
        gate, up = partial_sums(group, p)
        core_out[i, :, :piece] = gate.astype(bf16)
        core_out[i, :, piece:] = up.astype(bf16)
        return push(core_out.at[i], core_in.at[i], core_send.at[i], core_recv.at[i], core_peer)

    def add_core(i, copy, gate, up):
        copy.wait_recv()
        return gate + core_in[i, :, :piece].astype(f32), up + core_in[i, :, piece:].astype(f32)

    def to_y(group):
        copy = to_core(group, group, far_l)
        gate, up = add_core(group, copy, *partial_sums(group, y_peer_l))
        y_out[group, :, :piece] = gate.astype(bf16)
        y_out[group, :, piece:] = up.astype(bf16)
        return push(y_out.at[group], y_in.at[group], y_send.at[group], y_recv.at[group], y_peer)

    def spread(group, p, i, peer):
        return pltpu.make_async_remote_copy(
            src_ref=hid.at[group, p], dst_ref=hid.at[group, p], send_sem=hid_send.at[group, i],
            recv_sem=hid_recv.at[group, p], device_id=peer, device_id_type=MESH,
        )

    def activate(group, gate, up, over_y):
        over_y.wait_recv()
        gate = gate + y_in[group, :, :piece].astype(f32)
        up = up + y_in[group, :, piece:].astype(f32)
        hid[group, local] = (gate / (1.0 + jnp.exp(-gate)) * up).astype(bf16)
        for i, peer in enumerate((y_peer, far_peer, core_peer)):
            start(spread(group, local, i, peer))

    over_y0 = to_y(0)
    for pz in [z] + z_peers:
        gather(1 - x, pz, fw_send.at[0], x_peer).wait_recv()
    over_y1 = to_y(1)
    near0 = to_core(2, 0, core_peer_l)
    gate0, up0 = partial_sums(0, local)
    near1 = to_core(3, 1, core_peer_l)
    activate(0, *add_core(2, near0, gate0, up0), over_y0)
    gate1, up1 = partial_sums(1, local)
    activate(1, *add_core(3, near1, gate1, up1), over_y1)
    loads[6].wait()

    chunk_at = [slice(j * cols, (j + 1) * cols) for j in range(CHUNKS)]

    def down(group, p, where):
        depth = pl.ds(pl.multiple_of(p * piece, piece), piece)
        return jnp.dot(hid[group, p], dw[depth, where], preferred_element_type=f32)

    lane = lax.broadcasted_iota(jnp.int32, (half, LANES), 1)
    mine = (lane == node) | (lane == node + nodes) | (lane == node + 2 * nodes)

    def give_back(group):
        for where in chunk_at:
            acc[group, :, where] = down(group, local, where)
        for p in (core_peer_l, y_peer_l):
            spread(group, p, 0, core_peer).wait_recv()
            for where in chunk_at:
                acc[group, :, where] += down(group, p, where)
        coded = arr[planes[group], :, :, width:].reshape(half, LANES).astype(f32)
        weight = jnp.sum(jnp.where(mine, coded, 0.0), axis=1, keepdims=True)
        spread(group, far_l, 0, core_peer).wait_recv()
        targets = ([z] + z_peers, other_plane) if group else (z_peers, same_plane)
        for j, where in enumerate(chunk_at):
            result = (acc[group, :, where] + down(group, far_l, where)).astype(bf16).astype(f32)
            weighted = (result * weight).reshape(nz, rows, cols)
            back_out[group, j] = weighted.astype(bf16)
            if group == 0:
                own[j] = weighted
            for i, (pz, peer) in enumerate(zip(*targets)):
                slot = i + group * (nz - 1)
                push(back_out.at[group, j, pz], back_in.at[j, slot],
                     back_send.at[j, slot], back_recv.at[j, slot], peer)

    give_back(0)
    give_back(1)

    for j, where in enumerate(chunk_at):
        mixed = own[j, z]
        for i in range(nodes - 1):
            pltpu.make_async_remote_copy(
                src_ref=back_out.at[0, j, 0], dst_ref=back_in.at[j, i], send_sem=back_send.at[j, i],
                recv_sem=back_recv.at[j, i], device_id=x_peer, device_id_type=MESH,
            ).wait_recv()
            mixed = mixed + back_in[j, i].astype(f32)
        out_ref[:, where] = mixed.astype(bf16)

    for copy in sent:
        copy.wait_send()


def fused(tokens, sign_bits, routes, gate_values, gate_w, up_w, down_w):
    nodes = lax.axis_size("node")
    rows, width = tokens.shape
    hidden = gate_w.shape[2]
    nz, piece, cols = nodes // 2, hidden // 4, width // CHUNKS
    total, half = nodes * rows, nz * rows
    bf16, f32 = jnp.bfloat16, jnp.float32
    dma = pltpu.SemaphoreType.DMA
    vmem = pl.BlockSpec(memory_space=pltpu.VMEM)
    hbm = pl.BlockSpec(memory_space=pltpu.HBM)
    return pl.pallas_call(
        functools.partial(fused_kernel, nodes),
        out_shape=pltpu.VMEM((rows, width), bf16),
        in_specs=[hbm] * 7,
        out_specs=vmem,
        scratch_shapes=[
            pltpu.VMEM((rows, width), bf16),
            pltpu.VMEM((1, width), jnp.int32),
            pltpu.VMEM((routes.shape[1], rows), jnp.int32),
            pltpu.VMEM((routes.shape[1], rows), f32),
            pltpu.VMEM((width, hidden), bf16),
            pltpu.VMEM((width, hidden), bf16),
            pltpu.VMEM((hidden, width), bf16),
            pltpu.VMEM((2, nz, rows, width + LANES), bf16),
            pltpu.VMEM((4, half, 2 * piece), bf16),
            pltpu.VMEM((4, half, 2 * piece), bf16),
            pltpu.VMEM((2, half, 2 * piece), bf16),
            pltpu.VMEM((2, half, 2 * piece), bf16),
            pltpu.VMEM((2, 4, half, piece), bf16),
            pltpu.VMEM((2, half, width), f32),
            pltpu.VMEM((CHUNKS, nz, rows, cols), f32),
            pltpu.VMEM((2, CHUNKS, nz, rows, cols), bf16),
            pltpu.VMEM((CHUNKS, nodes - 1, rows, cols), bf16),
            dma((7,)),
            dma((nz - 1,)), dma((2, nz)), dma((nz,)),
            dma((4,)), dma((4,)), dma((2,)), dma((2,)),
            dma((2, 3)), dma((2, 4)),
            dma((CHUNKS, nodes - 1)), dma((CHUNKS, nodes - 1)),
        ],
        compiler_params=pltpu.CompilerParams(
            collective_id=0, has_side_effects=True, vmem_limit_bytes=VMEM_BYTES
        ),
        cost_estimate=pl.CostEstimate(
            flops=6 * total * width * hidden, bytes_accessed=6 * width * hidden, transcendentals=0
        ),
    )(tokens, sign_bits.reshape(1, width), routes.T, gate_values.T, gate_w, up_w, down_w)


def fits_fused(tokens, routes, gate_w, capacity):
    nodes, rows = lax.axis_size("node"), tokens.shape[0]
    return (
        capacity >= rows
        and nodes % 2 == 0
        and 4 <= nodes <= 16
        and lax.axis_size("local") == 4
        and rows % 16 == 0
        and nodes * rows <= 256
        and tokens.shape[1] % (CHUNKS * LANES) == 0
        and gate_w.shape[2] % (4 * LANES) == 0
    )


def hadamard_table(block_order):
    kernel_two = jnp.array([[1.0, 1.0], [1.0, -1.0]], jnp.float32)
    matrix = jnp.ones((1, 1), jnp.float32)
    while matrix.shape[0] < block_order:
        matrix = jnp.kron(matrix, kernel_two)
    return matrix / math.sqrt(block_order)


def slot_table(routes, experts, capacity):
    rows_all = routes.shape[0] * routes.shape[1]
    flat_routes = routes.reshape(rows_all)
    onehot = (flat_routes[:, None] == jnp.arange(experts, dtype=jnp.int32)[None, :]).astype(
        jnp.int32
    )
    ranks = jnp.sum(jnp.cumsum(onehot, axis=0) * onehot, axis=1) - 1
    slot_ids = flat_routes * capacity + ranks
    return slot_ids[None, :] == jnp.arange(experts * capacity, dtype=jnp.int32)[:, None]


def per_device(tokens, sign_bits, routes, gate_values, gate_w, up_w, down_w):
    experts = lax.axis_size("node")
    tok_node, width_dev = tokens.shape
    top_count = routes.shape[1]
    capacity = max(2, 2 * tok_node * top_count // experts)
    if fits_fused(tokens, routes, gate_w, capacity):
        return fused(tokens, sign_bits, routes, gate_values, gate_w, up_w, down_w)
    placed = slot_table(routes, experts, capacity).reshape(experts * capacity, tok_node, top_count)
    scatter_mat = jnp.any(placed, axis=2).astype(jnp.bfloat16)
    combine_mat = jnp.sum(placed.astype(jnp.float32) * gate_values[None, :, :], axis=2)
    hadamard = hadamard_table(HB)
    sign_vals = (1 - 2 * sign_bits).astype(jnp.float32)
    signed = tokens.astype(jnp.float32) * sign_vals[None, :]
    block_count = width_dev // HB
    group_size = min(2, block_count)
    group_width = group_size * HB
    received = []
    for group_index in range(block_count // group_size):
        rotated_parts = []
        for inner_index in range(group_size):
            first_col = group_index * group_width + inner_index * HB
            feature_block = signed[:, first_col : first_col + HB]
            rotated_parts.append(
                jnp.dot(feature_block, hadamard, precision=lax.Precision.HIGHEST).astype(
                    jnp.bfloat16
                )
            )
        rotated = jnp.concatenate(rotated_parts, axis=1)
        outgoing = jnp.dot(scatter_mat, rotated, preferred_element_type=jnp.float32).astype(
            jnp.bfloat16
        )
        received.append(lax.all_to_all(outgoing, "node", split_axis=0, concat_axis=0, tiled=True))
    arrived = jnp.concatenate(received, axis=1)
    gate_part = jnp.dot(arrived, gate_w[0], preferred_element_type=jnp.float32)
    up_part = jnp.dot(arrived, up_w[0], preferred_element_type=jnp.float32)
    gate_full, up_full = lax.psum((gate_part, up_part), "local")
    hidden_full = (jax.nn.silu(gate_full) * up_full).astype(jnp.bfloat16)
    expert_sum = jnp.dot(hidden_full, down_w[0], preferred_element_type=jnp.float32)
    expert_out = expert_sum.astype(jnp.bfloat16)
    combine_left = combine_mat.T
    mixed_blocks = []
    for group_index in range(block_count // group_size):
        out_block = expert_out[:, group_index * group_width : (group_index + 1) * group_width]
        returned_rows = lax.all_to_all(out_block, "node", split_axis=0, concat_axis=0, tiled=True)
        mixed_blocks.append(
            jnp.dot(
                combine_left, returned_rows.astype(jnp.float32), precision=lax.Precision.HIGHEST
            )
        )
    return jnp.concatenate(mixed_blocks, axis=1).astype(jnp.bfloat16)


def solution(mesh):
    in_specs = (
        P("node", "local"),
        P("local"),
        P("node", None),
        P("node", None),
        P("node", "local", None),
        P("node", "local", None),
        P("node", None, "local"),
    )
    out_specs = P("node", "local")
    return jax.shard_map(
        per_device, mesh=mesh, in_specs=in_specs, out_specs=out_specs, check_vma=False
    )
```

time: 35.1 us -> 30.5 us (0.87)
  Pallas kernels: 33.6 us -> 29.7 us
  local copies, waits for them, and re-layouts: 1.38 us -> 0.62 us
    pallas_call x1, Pallas kernels: 33.6 us -> 29.7 us  [fused(): pl.pallas_call(functools.partial(fused_kernel, nodes), out_shape=pltpu.VM...]
    unnamed x1, local copies, waits for them, and re-layouts: 1.38 us -> 0.62 us
where the time goes in v3:
time: 30.5 us; the launch traced here: 30.4 us
  Pallas kernels  29.7 us (97%)
  local copies, waits for them, and re-layouts  0.62 us (2%)
    pallas_call x1, Pallas kernels, fused(): pl.pallas_call(functools.partial(fused_kernel, nodes), out_shape=pltpu.VM...  29.7 us
    unnamed x1, local copies, waits for them, and re-layouts  0.62 us

profile of v3, /device:TPU:0, one launch (start us, length us, event | category | flops | bytes accessed | tf_op | source)
XLA Modules:
  0.0 30.4 jit_solution(16651958412338565081)
XLA Ops:
  0.0 29.7 %shard_map.73 = bf16[16,1024]{1,0:T(8,128)(2,1)S(1)} custom-call(bf16[16,1024]{1,0:T(8,128)(2,1)} %tok_hbm.1, s32[1,1024]{1,0:T(1,128)} %bitcast.3, s32[4,16]{1,0:T(4,128)} %bitcast.4, f32[4,16]{1,0:T(4,128)} %bitcast.5, bf16[1,1024,1024]{2,1,0:T(8,128)(2,1)} %gw_hbm.1, bf16[1,1024,1024]{2,1,0:T(8,128)(2,1)} %uw_hbm.1, bf16[1,1024,1024]{2,1,0:T(8,128)(2,1)} %dw_hbm.1), custom_call_target="tpu_custom_call" | custom-call | flops 805306368 | bytes 6291456 | tf_op jit(solution)/shard_map/pallas_call | solution.py:229
  29.7 0.6 %copy.9 = bf16[16,1024]{1,0:T(8,128)(2,1)} copy(bf16[16,1024]{1,0:T(8,128)(2,1)S(1)} %shard_map.73) | data formatting | bytes 65536

commit v4 on v3

--- a/solution.py
+++ b/solution.py
@@ -35,14 +35,14 @@
     z, x = node // 2, node % 2
     y, c = local // 2, local % 2
     x_peer = {"node": z * 2 + (1 - x)}
-    z_peers = [(z + step) % nz for step in range(1, nz)]
+    z_peers = [z + 1 - 2 * (z % 2), (z + 2) % nz, nz - 1 - z]
     core_peer_l, y_peer_l, far_l = y * 2 + (1 - c), (1 - y) * 2 + c, (1 - y) * 2 + (1 - c)
     core_peer, y_peer, far_peer = {"local": core_peer_l}, {"local": y_peer_l}, {"local": far_l}
     same_plane = [{"node": pz * 2 + x} for pz in z_peers]
     other_plane = [{"node": pz * 2 + (1 - x)} for pz in [z] + z_peers]
 
     barrier = pltpu.get_barrier_semaphore()
-    peers = [core_peer, y_peer, far_peer] + same_plane + other_plane
+    peers = [core_peer, y_peer, x_peer] + same_plane
     for peer in peers:
         pl.semaphore_signal(barrier, inc=1, device_id=peer, device_id_type=MESH)
 
@@ -106,8 +106,8 @@
             device_id=peer, device_id_type=MESH,
         ))
 
-    for i, peer in enumerate(same_plane):
-        start(gather(x, z, ag_send.at[i], peer))
+    for i in (1, 2, 0):
+        start(gather(x, z, ag_send.at[i], same_plane[i]))
     start(gather(x, z, fw_send.at[nz - 1], x_peer))
     for i, pz in enumerate(z_peers):
         copy = gather(x, pz, fw_send.at[i], x_peer)
@@ -157,10 +157,10 @@
             start(spread(group, local, i, peer))
 
     over_y0 = to_y(0)
+    near0 = to_core(2, 0, core_peer_l)
     for pz in [z] + z_peers:
         gather(1 - x, pz, fw_send.at[0], x_peer).wait_recv()
     over_y1 = to_y(1)
-    near0 = to_core(2, 0, core_peer_l)
     gate0, up0 = partial_sums(0, local)
     near1 = to_core(3, 1, core_peer_l)
     activate(0, *add_core(2, near0, gate0, up0), over_y0)
@@ -201,6 +201,8 @@
 
     give_back(0)
     give_back(1)
+    for copy in sent:
+        copy.wait_send()
 
     for j, where in enumerate(chunk_at):
         mixed = own[j, z]
@@ -211,9 +213,6 @@
             ).wait_recv()
             mixed = mixed + back_in[j, i].astype(f32)
         out_ref[:, where] = mixed.astype(bf16)
-
-    for copy in sent:
-        copy.wait_send()
 
 
 def fused(tokens, sign_bits, routes, gate_values, gate_w, up_w, down_w):
@@ -268,8 +267,7 @@
     nodes, rows = lax.axis_size("node"), tokens.shape[0]
     return (
         capacity >= rows
-        and nodes % 2 == 0
-        and 4 <= nodes <= 16
+        and nodes == 8
         and lax.axis_size("local") == 4
         and rows % 16 == 0
         and nodes * rows <= 256

time: 30.5 us -> 29 us (0.951)
  Pallas kernels: 29.7 us -> 28.2 us
    pallas_call x1, Pallas kernels: 29.7 us -> 28.2 us  [fused(): pl.pallas_call(functools.partial(fused_kernel, nodes), out_shape=pltpu.VM...]
where the time goes in v4:
time: 29 us; the launch traced here: 28.9 us
  Pallas kernels  28.2 us (97%)
  local copies, waits for them, and re-layouts  0.62 us (2%)
    pallas_call x1, Pallas kernels, fused(): pl.pallas_call(functools.partial(fused_kernel, nodes), out_shape=pltpu.VM...  28.2 us
    unnamed x1, local copies, waits for them, and re-layouts  0.62 us

profile of v4, /device:TPU:0, one launch (start us, length us, event | category | flops | bytes accessed | tf_op | source)
XLA Modules:
  0.0 28.9 jit_solution(18043965106474771157)
XLA Ops:
  0.0 28.2 %shard_map.73 = bf16[16,1024]{1,0:T(8,128)(2,1)S(1)} custom-call(bf16[16,1024]{1,0:T(8,128)(2,1)} %tok_hbm.1, s32[1,1024]{1,0:T(1,128)} %bitcast.3, s32[4,16]{1,0:T(4,128)} %bitcast.4, f32[4,16]{1,0:T(4,128)} %bitcast.5, bf16[1,1024,1024]{2,1,0:T(8,128)(2,1)} %gw_hbm.1, bf16[1,1024,1024]{2,1,0:T(8,128)(2,1)} %uw_hbm.1, bf16[1,1024,1024]{2,1,0:T(8,128)(2,1)} %dw_hbm.1), custom_call_target="tpu_custom_call" | custom-call | flops 805306368 | bytes 6291456 | tf_op jit(solution)/shard_map/pallas_call | solution.py:228
  28.3 0.6 %copy.9 = bf16[16,1024]{1,0:T(8,128)(2,1)} copy(bf16[16,1024]{1,0:T(8,128)(2,1)S(1)} %shard_map.73) | data formatting | bytes 65536

commit v5 on v4

--- a/solution.py
+++ b/solution.py
@@ -18,9 +18,9 @@
 def fused_kernel(
     nodes,
     tok_hbm, sign_hbm, routes_hbm, gv_hbm, gw_hbm, uw_hbm, dw_hbm, out_ref,
-    tok_ref, sign_ref, routes_ref, gv_ref, gw, uw, dw, arr,
+    tok_ref, sign_ref, routes_ref, gv_ref, gw, uw, dw, arr, gates,
     core_out, core_in, y_out, y_in, hid, acc, own, back_out, back_in,
-    w_sem, ag_send, ag_recv, fw_send, core_send, core_recv, y_send, y_recv,
+    w_sem, ag_send, ag_recv, fw_send, gate_send, gate_recv, core_send, core_recv, y_send, y_recv,
     hid_send, hid_recv, back_send, back_recv,
 ):
     rows, width = tok_hbm.shape
@@ -62,13 +62,96 @@
     bits = bits ^ (bits >> 2)
     bits = bits ^ (bits >> 1)
     table = (1 - 2 * (bits & 1)).astype(f32).astype(bf16)
-    for load in loads[:4]:
-        load.wait()
+    loads[0].wait()
+    loads[1].wait()
     signs = (1 - 2 * sign_ref[...]).astype(f32)
     signed = (tok_ref[...].astype(f32) * signs).astype(bf16)
-    for b in range(width // HB):
-        block = jnp.dot(signed[:, b * HB : (b + 1) * HB], table, preferred_element_type=f32)
-        arr[x, z, :, b * HB : (b + 1) * HB] = (block * (1.0 / math.sqrt(HB))).astype(bf16)
+    count = width // HB
+    stacked = jnp.concatenate([signed[:, b * HB : (b + 1) * HB] for b in range(count)], axis=0)
+    turned = jnp.dot(stacked, table, preferred_element_type=f32) * (1.0 / math.sqrt(HB))
+    for b in range(count):
+        arr[x, z, :, b * HB : (b + 1) * HB] = turned[b * rows : (b + 1) * rows].astype(bf16)
+
+    pl.semaphore_wait(barrier, len(peers))
+
+    def gather(plane, pz, send_sem, peer):
+        return pltpu.make_async_remote_copy(
+            src_ref=arr.at[plane, pz], dst_ref=arr.at[plane, pz], send_sem=send_sem,
+            recv_sem=ag_recv.at[plane, pz], device_id=peer, device_id_type=MESH,
+        )
+
+    sent = []
+
+    def start(copy):
+        copy.start()
+        sent.append(copy)
+        return copy
+
+    def push(src, dst, send_sem, recv_sem, peer):
+        return start(pltpu.make_async_remote_copy(
+            src_ref=src, dst_ref=dst, send_sem=send_sem, recv_sem=recv_sem,
+            device_id=peer, device_id_type=MESH,
+        ))
+
+    for i in (1, 2, 0):
+        start(gather(x, z, ag_send.at[i], same_plane[i]))
+    start(gather(x, z, fw_send.at[nz - 1], x_peer))
+    for i, pz in enumerate(z_peers):
+        copy = gather(x, pz, fw_send.at[i], x_peer)
+        copy.wait_recv()
+        start(copy)
+    loads[4].wait()
+    loads[5].wait()
+
+    planes = (x, 1 - x)
+
+    def partial_sums(group, p):
+        where = pl.ds(pl.multiple_of(p * piece, piece), piece)
+        tokens = arr[planes[group]].reshape(half, width)
+        gate = jnp.dot(tokens, gw[:, where], preferred_element_type=f32)
+        up = jnp.dot(tokens, uw[:, where], preferred_element_type=f32)
+        return gate, up
+
+    def to_core(i, group, p):
+        gate, up = partial_sums(group, p)
+        core_out[i, :, :piece] = gate.astype(bf16)
+        core_out[i, :, piece:] = up.astype(bf16)
+        return push(core_out.at[i], core_in.at[i], core_send.at[i], core_recv.at[i], core_peer)
+
+    def add_core(i, copy, gate, up):
+        copy.wait_recv()
+        return gate + core_in[i, :, :piece].astype(f32), up + core_in[i, :, piece:].astype(f32)
+
+    def to_y(group):
+        copy = to_core(group, group, far_l)
+        gate, up = add_core(group, copy, *partial_sums(group, y_peer_l))
+        y_out[group, :, :piece] = gate.astype(bf16)
+        y_out[group, :, piece:] = up.astype(bf16)
+        return push(y_out.at[group], y_in.at[group], y_send.at[group], y_recv.at[group], y_peer)
+
+    def spread(group, p, i, peer):
+        return pltpu.make_async_remote_copy(
+            src_ref=hid.at[group, p], dst_ref=hid.at[group, p], send_sem=hid_send.at[group, i],
+            recv_sem=hid_recv.at[group, p], device_id=peer, device_id_type=MESH,
+        )
+
+    def activate(group, gate, up, over_y):
+        over_y.wait_recv()
+        gate = gate + y_in[group, :, :piece].astype(f32)
+        up = up + y_in[group, :, piece:].astype(f32)
+        hid[group, local] = (gate / (1.0 + jnp.exp(-gate)) * up).astype(bf16)
+        for i, peer in enumerate((y_peer, far_peer, core_peer)):
+            start(spread(group, local, i, peer))
+
+    over_y0 = to_y(0)
+    near0 = to_core(2, 0, core_peer_l)
+    for pz in [z] + z_peers:
+        gather(1 - x, pz, fw_send.at[0], x_peer).wait_recv()
+    over_y1 = to_y(1)
+    gate0, up0 = partial_sums(0, local)
+
+    loads[2].wait()
+    loads[3].wait()
     code = lax.broadcasted_iota(jnp.int32, (LANES, rows), 0)
     dense = jnp.zeros((LANES, rows), f32)
     for k in range(routes_ref.shape[0]):
@@ -83,87 +166,12 @@
     turned = lax.dot_general(
         same.astype(f32).astype(bf16), parts, (((1,), (1,)), ((), ())), preferred_element_type=f32
     )
-    arr[x, z, :, width:] = turned.astype(bf16)
-
-    pl.semaphore_wait(barrier, len(peers))
-
-    def gather(plane, pz, send_sem, peer):
-        return pltpu.make_async_remote_copy(
-            src_ref=arr.at[plane, pz], dst_ref=arr.at[plane, pz], send_sem=send_sem,
-            recv_sem=ag_recv.at[plane, pz], device_id=peer, device_id_type=MESH,
-        )
-
-    sent = []
-
-    def start(copy):
-        copy.start()
-        sent.append(copy)
-        return copy
-
-    def push(src, dst, send_sem, recv_sem, peer):
-        return start(pltpu.make_async_remote_copy(
-            src_ref=src, dst_ref=dst, send_sem=send_sem, recv_sem=recv_sem,
-            device_id=peer, device_id_type=MESH,
-        ))
-
-    for i in (1, 2, 0):
-        start(gather(x, z, ag_send.at[i], same_plane[i]))
-    start(gather(x, z, fw_send.at[nz - 1], x_peer))
-    for i, pz in enumerate(z_peers):
-        copy = gather(x, pz, fw_send.at[i], x_peer)
-        copy.wait_recv()
-        start(copy)
-    loads[4].wait()
-    loads[5].wait()
-
-    planes = (x, 1 - x)
-
-    def partial_sums(group, p):
-        where = pl.ds(pl.multiple_of(p * piece, piece), piece)
-        tokens = arr[planes[group], :, :, :width].reshape(half, width)
-        gate = jnp.dot(tokens, gw[:, where], preferred_element_type=f32)
-        up = jnp.dot(tokens, uw[:, where], preferred_element_type=f32)
-        return gate, up
-
-    def to_core(i, group, p):
-        gate, up = partial_sums(group, p)
-        core_out[i, :, :piece] = gate.astype(bf16)
-        core_out[i, :, piece:] = up.astype(bf16)
-        return push(core_out.at[i], core_in.at[i], core_send.at[i], core_recv.at[i], core_peer)
-
-    def add_core(i, copy, gate, up):
-        copy.wait_recv()
-        return gate + core_in[i, :, :piece].astype(f32), up + core_in[i, :, piece:].astype(f32)
-
-    def to_y(group):
-        copy = to_core(group, group, far_l)
-        gate, up = add_core(group, copy, *partial_sums(group, y_peer_l))
-        y_out[group, :, :piece] = gate.astype(bf16)
-        y_out[group, :, piece:] = up.astype(bf16)
-        return push(y_out.at[group], y_in.at[group], y_send.at[group], y_recv.at[group], y_peer)
-
-    def spread(group, p, i, peer):
-        return pltpu.make_async_remote_copy(
-            src_ref=hid.at[group, p], dst_ref=hid.at[group, p], send_sem=hid_send.at[group, i],
-            recv_sem=hid_recv.at[group, p], device_id=peer, device_id_type=MESH,
-        )
-
-    def activate(group, gate, up, over_y):
-        over_y.wait_recv()
-        gate = gate + y_in[group, :, :piece].astype(f32)
-        up = up + y_in[group, :, piece:].astype(f32)
-        hid[group, local] = (gate / (1.0 + jnp.exp(-gate)) * up).astype(bf16)
-        for i, peer in enumerate((y_peer, far_peer, core_peer)):
-            start(spread(group, local, i, peer))
-
-    over_y0 = to_y(0)
-    near0 = to_core(2, 0, core_peer_l)
-    for pz in [z] + z_peers:
-        gather(1 - x, pz, fw_send.at[0], x_peer).wait_recv()
-    over_y1 = to_y(1)
-    gate0, up0 = partial_sums(0, local)
+    gates[x, z] = turned.astype(bf16)
+    for i, peer in enumerate(same_plane + other_plane):
+        push(gates.at[x, z], gates.at[x, z], gate_send.at[i], gate_recv.at[x, z], peer)
+
+    activate(0, *add_core(2, near0, gate0, up0), over_y0)
     near1 = to_core(3, 1, core_peer_l)
-    activate(0, *add_core(2, near0, gate0, up0), over_y0)
     gate1, up1 = partial_sums(1, local)
     activate(1, *add_core(3, near1, gate1, up1), over_y1)
     loads[6].wait()
@@ -184,7 +192,12 @@
             spread(group, p, 0, core_peer).wait_recv()
             for where in chunk_at:
                 acc[group, :, where] += down(group, p, where)
-        coded = arr[planes[group], :, :, width:].reshape(half, LANES).astype(f32)
+        for pz in z_peers + ([z] if group else []):
+            pltpu.make_async_remote_copy(
+                src_ref=gates.at[x, z], dst_ref=gates.at[planes[group], pz], send_sem=gate_send.at[0],
+                recv_sem=gate_recv.at[planes[group], pz], device_id=x_peer, device_id_type=MESH,
+            ).wait_recv()
+        coded = gates[planes[group]].reshape(half, LANES).astype(f32)
         weight = jnp.sum(jnp.where(mine, coded, 0.0), axis=1, keepdims=True)
         spread(group, far_l, 0, core_peer).wait_recv()
         targets = ([z] + z_peers, other_plane) if group else (z_peers, same_plane)
@@ -194,7 +207,8 @@
             back_out[group, j] = weighted.astype(bf16)
             if group == 0:
                 own[j] = weighted
-            for i, (pz, peer) in enumerate(zip(*targets)):
+            for i in ((2, 3, 1, 0) if group else (1, 2, 0)):
+                pz, peer = targets[0][i], targets[1][i]
                 slot = i + group * (nz - 1)
                 push(back_out.at[group, j, pz], back_in.at[j, slot],
                      back_send.at[j, slot], back_recv.at[j, slot], peer)
@@ -238,7 +252,8 @@
             pltpu.VMEM((width, hidden), bf16),
             pltpu.VMEM((width, hidden), bf16),
             pltpu.VMEM((hidden, width), bf16),
-            pltpu.VMEM((2, nz, rows, width + LANES), bf16),
+            pltpu.VMEM((2, nz, rows, width), bf16),
+            pltpu.VMEM((2, nz, rows, LANES), bf16),
             pltpu.VMEM((4, half, 2 * piece), bf16),
             pltpu.VMEM((4, half, 2 * piece), bf16),
             pltpu.VMEM((2, half, 2 * piece), bf16),
@@ -249,7 +264,7 @@
             pltpu.VMEM((2, CHUNKS, nz, rows, cols), bf16),
             pltpu.VMEM((CHUNKS, nodes - 1, rows, cols), bf16),
             dma((7,)),
-            dma((nz - 1,)), dma((2, nz)), dma((nz,)),
+            dma((nz - 1,)), dma((2, nz)), dma((nz,)), dma((nodes - 1,)), dma((2, nz)),
             dma((4,)), dma((4,)), dma((2,)), dma((2,)),
             dma((2, 3)), dma((2, 4)),
             dma((CHUNKS, nodes - 1)), dma((CHUNKS, nodes - 1)),

time: 29 us -> 28.9 us (level)
  no operation moved by 1% of the time
where the time goes in v5:
time: 28.9 us; the launch traced here: 28.8 us
  Pallas kernels  28.2 us (98%)
  local copies, waits for them, and re-layouts  0.62 us (2%)
    pallas_call x1, Pallas kernels, fused(): pl.pallas_call(functools.partial(fused_kernel, nodes), out_shape=pltpu.VM...  28.2 us
    unnamed x1, local copies, waits for them, and re-layouts  0.62 us

profile of v5, /device:TPU:0, one launch (start us, length us, event | category | flops | bytes accessed | tf_op | source)
XLA Modules:
  0.0 28.8 jit_solution(11217601768529349213)
XLA Ops:
  0.0 28.2 %shard_map.73 = bf16[16,1024]{1,0:T(8,128)(2,1)S(1)} custom-call(bf16[16,1024]{1,0:T(8,128)(2,1)} %tok_hbm.1, s32[1,1024]{1,0:T(1,128)} %bitcast.3, s32[4,16]{1,0:T(4,128)} %bitcast.4, f32[4,16]{1,0:T(4,128)} %bitcast.5, bf16[1,1024,1024]{2,1,0:T(8,128)(2,1)} %gw_hbm.1, bf16[1,1024,1024]{2,1,0:T(8,128)(2,1)} %uw_hbm.1, bf16[1,1024,1024]{2,1,0:T(8,128)(2,1)} %dw_hbm.1), custom_call_target="tpu_custom_call" | custom-call | flops 805306368 | bytes 6291456 | tf_op jit(solution)/shard_map/pallas_call | solution.py:242
  28.2 0.6 %copy.9 = bf16[16,1024]{1,0:T(8,128)(2,1)} copy(bf16[16,1024]{1,0:T(8,128)(2,1)S(1)} %shard_map.73) | data formatting | bytes 65536

commit v6 on v5

--- a/solution.py
+++ b/solution.py
@@ -10,7 +10,7 @@
 
 HB = 128
 LANES = 128
-CHUNKS = 2
+CHUNKS = 1
 VMEM_BYTES = 63 * 1024 * 1024
 MESH = pl.DeviceIdType.MESH
 
@@ -25,7 +25,7 @@
 ):
     rows, width = tok_hbm.shape
     nz = nodes // 2
-    half = nz * rows
+    part = 2 * rows
     piece = gw.shape[1] // 4
     cols = width // CHUNKS
     f32, bf16 = jnp.float32, jnp.bfloat16
@@ -70,13 +70,13 @@
     stacked = jnp.concatenate([signed[:, b * HB : (b + 1) * HB] for b in range(count)], axis=0)
     turned = jnp.dot(stacked, table, preferred_element_type=f32) * (1.0 / math.sqrt(HB))
     for b in range(count):
-        arr[x, z, :, b * HB : (b + 1) * HB] = turned[b * rows : (b + 1) * rows].astype(bf16)
+        arr[x, z // 2, z % 2, :, b * HB : (b + 1) * HB] = turned[b * rows : (b + 1) * rows].astype(bf16)
 
     pl.semaphore_wait(barrier, len(peers))
 
     def gather(plane, pz, send_sem, peer):
         return pltpu.make_async_remote_copy(
-            src_ref=arr.at[plane, pz], dst_ref=arr.at[plane, pz], send_sem=send_sem,
+            src_ref=arr.at[plane, pz // 2, pz % 2], dst_ref=arr.at[plane, pz // 2, pz % 2], send_sem=send_sem,
             recv_sem=ag_recv.at[plane, pz], device_id=peer, device_id_type=MESH,
         )
 
@@ -96,18 +96,19 @@
     for i in (1, 2, 0):
         start(gather(x, z, ag_send.at[i], same_plane[i]))
     start(gather(x, z, fw_send.at[nz - 1], x_peer))
-    for i, pz in enumerate(z_peers):
-        copy = gather(x, pz, fw_send.at[i], x_peer)
+
+    def relay(i):
+        copy = gather(x, z_peers[i], fw_send.at[i], x_peer)
         copy.wait_recv()
         start(copy)
-    loads[4].wait()
-    loads[5].wait()
-
-    planes = (x, 1 - x)
+
+    near, far = z // 2, 1 - z // 2
+    groups = ((x, near), (x, far), (1 - x, far), (1 - x, near))
+    group_z = ((z, z_peers[0]), z_peers[1:], z_peers[1:], (z, z_peers[0]))
 
     def partial_sums(group, p):
         where = pl.ds(pl.multiple_of(p * piece, piece), piece)
-        tokens = arr[planes[group]].reshape(half, width)
+        tokens = arr[groups[group]].reshape(part, width)
         gate = jnp.dot(tokens, gw[:, where], preferred_element_type=f32)
         up = jnp.dot(tokens, uw[:, where], preferred_element_type=f32)
         return gate, up
@@ -122,12 +123,19 @@
         copy.wait_recv()
         return gate + core_in[i, :, :piece].astype(f32), up + core_in[i, :, piece:].astype(f32)
 
-    def to_y(group):
-        copy = to_core(group, group, far_l)
-        gate, up = add_core(group, copy, *partial_sums(group, y_peer_l))
+    def first_piece(group):
+        copy = to_core(2 * group, group, far_l)
+        return (2 * group, copy, *partial_sums(group, y_peer_l))
+
+    def to_y(group, begun):
+        gate, up = add_core(*begun)
         y_out[group, :, :piece] = gate.astype(bf16)
         y_out[group, :, piece:] = up.astype(bf16)
         return push(y_out.at[group], y_in.at[group], y_send.at[group], y_recv.at[group], y_peer)
+
+    def own_piece(group):
+        copy = to_core(2 * group + 1, group, core_peer_l)
+        return (2 * group + 1, copy, *partial_sums(group, local))
 
     def spread(group, p, i, peer):
         return pltpu.make_async_remote_copy(
@@ -135,7 +143,8 @@
             recv_sem=hid_recv.at[group, p], device_id=peer, device_id_type=MESH,
         )
 
-    def activate(group, gate, up, over_y):
+    def activate(group, begun, over_y):
+        gate, up = add_core(*begun)
         over_y.wait_recv()
         gate = gate + y_in[group, :, :piece].astype(f32)
         up = up + y_in[group, :, piece:].astype(f32)
@@ -143,12 +152,27 @@
         for i, peer in enumerate((y_peer, far_peer, core_peer)):
             start(spread(group, local, i, peer))
 
-    over_y0 = to_y(0)
-    near0 = to_core(2, 0, core_peer_l)
-    for pz in [z] + z_peers:
+    relay(0)
+    loads[4].wait()
+    loads[5].wait()
+    first0 = first_piece(0)
+    relay(1)
+    relay(2)
+    over_y0 = to_y(0, first0)
+    first1 = first_piece(1)
+    own0 = own_piece(0)
+    over_y1 = to_y(1, first1)
+    for pz in group_z[2]:
         gather(1 - x, pz, fw_send.at[0], x_peer).wait_recv()
-    over_y1 = to_y(1)
-    gate0, up0 = partial_sums(0, local)
+    first2 = first_piece(2)
+    own1 = own_piece(1)
+    over_y2 = to_y(2, first2)
+    for pz in group_z[3]:
+        gather(1 - x, pz, fw_send.at[0], x_peer).wait_recv()
+    first3 = first_piece(3)
+    activate(0, own0, over_y0)
+    over_y3 = to_y(3, first3)
+    own2 = own_piece(2)
 
     loads[2].wait()
     loads[3].wait()
@@ -166,14 +190,13 @@
     turned = lax.dot_general(
         same.astype(f32).astype(bf16), parts, (((1,), (1,)), ((), ())), preferred_element_type=f32
     )
-    gates[x, z] = turned.astype(bf16)
+    gates[x, near, z % 2] = turned.astype(bf16)
     for i, peer in enumerate(same_plane + other_plane):
-        push(gates.at[x, z], gates.at[x, z], gate_send.at[i], gate_recv.at[x, z], peer)
-
-    activate(0, *add_core(2, near0, gate0, up0), over_y0)
-    near1 = to_core(3, 1, core_peer_l)
-    gate1, up1 = partial_sums(1, local)
-    activate(1, *add_core(3, near1, gate1, up1), over_y1)
+        push(gates.at[x, near, z % 2], gates.at[x, near, z % 2], gate_send.at[i], gate_recv.at[x, z], peer)
+
+    activate(1, own1, over_y1)
+    own3 = own_piece(3)
+    activate(2, own2, over_y2)
     loads[6].wait()
 
     chunk_at = [slice(j * cols, (j + 1) * cols) for j in range(CHUNKS)]
@@ -182,7 +205,7 @@
         depth = pl.ds(pl.multiple_of(p * piece, piece), piece)
         return jnp.dot(hid[group, p], dw[depth, where], preferred_element_type=f32)
 
-    lane = lax.broadcasted_iota(jnp.int32, (half, LANES), 1)
+    lane = lax.broadcasted_iota(jnp.int32, (part, LANES), 1)
     mine = (lane == node) | (lane == node + nodes) | (lane == node + 2 * nodes)
 
     def give_back(group):
@@ -192,34 +215,36 @@
             spread(group, p, 0, core_peer).wait_recv()
             for where in chunk_at:
                 acc[group, :, where] += down(group, p, where)
-        for pz in z_peers + ([z] if group else []):
+        plane, pair = groups[group]
+        for pz in group_z[group][1 if group == 0 else 0 :]:
             pltpu.make_async_remote_copy(
-                src_ref=gates.at[x, z], dst_ref=gates.at[planes[group], pz], send_sem=gate_send.at[0],
-                recv_sem=gate_recv.at[planes[group], pz], device_id=x_peer, device_id_type=MESH,
+                src_ref=gates.at[x, near, z % 2], dst_ref=gates.at[plane, pair, pz % 2], send_sem=gate_send.at[0],
+                recv_sem=gate_recv.at[plane, pz], device_id=x_peer, device_id_type=MESH,
             ).wait_recv()
-        coded = gates[planes[group]].reshape(half, LANES).astype(f32)
+        coded = gates[plane, pair].reshape(part, LANES).astype(f32)
         weight = jnp.sum(jnp.where(mine, coded, 0.0), axis=1, keepdims=True)
         spread(group, far_l, 0, core_peer).wait_recv()
-        targets = ([z] + z_peers, other_plane) if group else (z_peers, same_plane)
         for j, where in enumerate(chunk_at):
             result = (acc[group, :, where] + down(group, far_l, where)).astype(bf16).astype(f32)
-            weighted = (result * weight).reshape(nz, rows, cols)
+            weighted = (result * weight).reshape(2, rows, cols)
             back_out[group, j] = weighted.astype(bf16)
             if group == 0:
                 own[j] = weighted
-            for i in ((2, 3, 1, 0) if group else (1, 2, 0)):
-                pz, peer = targets[0][i], targets[1][i]
-                slot = i + group * (nz - 1)
-                push(back_out.at[group, j, pz], back_in.at[j, slot],
+            for slot in ((0,), (1, 2), (5, 6), (4, 3))[group]:
+                pz, peer = ((z_peers + [z] + z_peers)[slot], (same_plane + other_plane)[slot])
+                push(back_out.at[group, j, pz % 2], back_in.at[j, slot],
                      back_send.at[j, slot], back_recv.at[j, slot], peer)
 
     give_back(0)
+    activate(3, own3, over_y3)
     give_back(1)
+    give_back(2)
+    give_back(3)
     for copy in sent:
         copy.wait_send()
 
     for j, where in enumerate(chunk_at):
-        mixed = own[j, z]
+        mixed = own[j, z % 2]
         for i in range(nodes - 1):
             pltpu.make_async_remote_copy(
                 src_ref=back_out.at[0, j, 0], dst_ref=back_in.at[j, i], send_sem=back_send.at[j, i],
@@ -234,7 +259,7 @@
     rows, width = tokens.shape
     hidden = gate_w.shape[2]
     nz, piece, cols = nodes // 2, hidden // 4, width // CHUNKS
-    total, half = nodes * rows, nz * rows
+    total, part = nodes * rows, 2 * rows
     bf16, f32 = jnp.bfloat16, jnp.float32
     dma = pltpu.SemaphoreType.DMA
     vmem = pl.BlockSpec(memory_space=pltpu.VMEM)
@@ -252,21 +277,21 @@
             pltpu.VMEM((width, hidden), bf16),
             pltpu.VMEM((width, hidden), bf16),
             pltpu.VMEM((hidden, width), bf16),
-            pltpu.VMEM((2, nz, rows, width), bf16),
-            pltpu.VMEM((2, nz, rows, LANES), bf16),
-            pltpu.VMEM((4, half, 2 * piece), bf16),
-            pltpu.VMEM((4, half, 2 * piece), bf16),
-            pltpu.VMEM((2, half, 2 * piece), bf16),
-            pltpu.VMEM((2, half, 2 * piece), bf16),
-            pltpu.VMEM((2, 4, half, piece), bf16),
-            pltpu.VMEM((2, half, width), f32),
-            pltpu.VMEM((CHUNKS, nz, rows, cols), f32),
-            pltpu.VMEM((2, CHUNKS, nz, rows, cols), bf16),
+            pltpu.VMEM((2, 2, 2, rows, width), bf16),
+            pltpu.VMEM((2, 2, 2, rows, LANES), bf16),
+            pltpu.VMEM((8, part, 2 * piece), bf16),
+            pltpu.VMEM((8, part, 2 * piece), bf16),
+            pltpu.VMEM((4, part, 2 * piece), bf16),
+            pltpu.VMEM((4, part, 2 * piece), bf16),
+            pltpu.VMEM((4, 4, part, piece), bf16),
+            pltpu.VMEM((4, part, width), f32),
+            pltpu.VMEM((CHUNKS, 2, rows, cols), f32),
+            pltpu.VMEM((4, CHUNKS, 2, rows, cols), bf16),
             pltpu.VMEM((CHUNKS, nodes - 1, rows, cols), bf16),
             dma((7,)),
             dma((nz - 1,)), dma((2, nz)), dma((nz,)), dma((nodes - 1,)), dma((2, nz)),
-            dma((4,)), dma((4,)), dma((2,)), dma((2,)),
-            dma((2, 3)), dma((2, 4)),
+            dma((8,)), dma((8,)), dma((4,)), dma((4,)),
+            dma((4, 3)), dma((4, 4)),
             dma((CHUNKS, nodes - 1)), dma((CHUNKS, nodes - 1)),
         ],
         compiler_params=pltpu.CompilerParams(

time: 28.9 us -> 29.5 us (1.021)
  Pallas kernels: 28.2 us -> 28.7 us
    pallas_call x1, Pallas kernels: 28.2 us -> 28.7 us  [fused(): pl.pallas_call(functools.partial(fused_kernel, nodes), out_shape=pltpu.VM...]
where the time goes in v6:
time: 29.5 us; the launch traced here: 29.3 us
  Pallas kernels  28.7 us (97%)
  local copies, waits for them, and re-layouts  0.62 us (2%)
    pallas_call x1, Pallas kernels, fused(): pl.pallas_call(functools.partial(fused_kernel, nodes), out_shape=pltpu.VM...  28.7 us
    unnamed x1, local copies, waits for them, and re-layouts  0.62 us

profile of v6, /device:TPU:0, one launch (start us, length us, event | category | flops | bytes accessed | tf_op | source)
XLA Modules:
  0.0 29.3 jit_solution(7682832023852161111)
XLA Ops:
  0.0 28.7 %shard_map.73 = bf16[16,1024]{1,0:T(8,128)(2,1)S(1)} custom-call(bf16[16,1024]{1,0:T(8,128)(2,1)} %tok_hbm.1, s32[1,1024]{1,0:T(1,128)} %bitcast.3, s32[4,16]{1,0:T(4,128)} %bitcast.4, f32[4,16]{1,0:T(4,128)} %bitcast.5, bf16[1,1024,1024]{2,1,0:T(8,128)(2,1)} %gw_hbm.1, bf16[1,1024,1024]{2,1,0:T(8,128)(2,1)} %uw_hbm.1, bf16[1,1024,1024]{2,1,0:T(8,128)(2,1)} %dw_hbm.1), custom_call_target="tpu_custom_call" | custom-call | flops 805306368 | bytes 6291456 | tf_op jit(solution)/shard_map/pallas_call | solution.py:267
  28.7 0.6 %copy.9 = bf16[16,1024]{1,0:T(8,128)(2,1)} copy(bf16[16,1024]{1,0:T(8,128)(2,1)S(1)} %shard_map.73) | data formatting | bytes 65536

commit v7 on v5

--- a/solution.py
+++ b/solution.py
@@ -27,6 +27,7 @@
     nz = nodes // 2
     half = nz * rows
     piece = gw.shape[1] // 4
+    sub = piece // 2
     cols = width // CHUNKS
     f32, bf16 = jnp.float32, jnp.bfloat16
 
@@ -104,6 +105,7 @@
     loads[5].wait()
 
     planes = (x, 1 - x)
+    halves = (((0,),), ((1, 0), (1, 1)))
 
     def partial_sums(group, p):
         where = pl.ds(pl.multiple_of(p * piece, piece), piece)
@@ -125,23 +127,37 @@
     def to_y(group):
         copy = to_core(group, group, far_l)
         gate, up = add_core(group, copy, *partial_sums(group, y_peer_l))
-        y_out[group, :, :piece] = gate.astype(bf16)
-        y_out[group, :, piece:] = up.astype(bf16)
-        return push(y_out.at[group], y_in.at[group], y_send.at[group], y_recv.at[group], y_peer)
-
-    def spread(group, p, i, peer):
+        for s in range(2):
+            y_out[group, s, :, :sub] = gate[:, s * sub : (s + 1) * sub].astype(bf16)
+            y_out[group, s, :, sub:] = up[:, s * sub : (s + 1) * sub].astype(bf16)
+        return [
+            push(y_out.at[part], y_in.at[part], y_send.at[group, s], y_recv.at[group, s], y_peer)
+            for s, part in enumerate(halves[group])
+        ]
+
+    def spread(group, s, p, i, peer):
+        part = halves[group][s]
+        ref = hid.at[p].at[part]
         return pltpu.make_async_remote_copy(
-            src_ref=hid.at[group, p], dst_ref=hid.at[group, p], send_sem=hid_send.at[group, i],
-            recv_sem=hid_recv.at[group, p], device_id=peer, device_id_type=MESH,
+            src_ref=ref, dst_ref=ref, send_sem=hid_send.at[group, s, i],
+            recv_sem=hid_recv.at[group, s, p], device_id=peer, device_id_type=MESH,
         )
 
     def activate(group, gate, up, over_y):
-        over_y.wait_recv()
-        gate = gate + y_in[group, :, :piece].astype(f32)
-        up = up + y_in[group, :, piece:].astype(f32)
-        hid[group, local] = (gate / (1.0 + jnp.exp(-gate)) * up).astype(bf16)
-        for i, peer in enumerate((y_peer, far_peer, core_peer)):
-            start(spread(group, local, i, peer))
+        share = 2 // len(over_y)
+        for s, copy in enumerate(over_y):
+            copy.wait_recv()
+            for t in range(s * share, (s + 1) * share):
+                cut = slice(t * sub, (t + 1) * sub)
+                g = gate[:, cut] + y_in[group, t, :, :sub].astype(f32)
+                u = up[:, cut] + y_in[group, t, :, sub:].astype(f32)
+                hid[local, group, t] = (g / (1.0 + jnp.exp(-g)) * u).astype(bf16)
+            for i, peer in enumerate((y_peer, far_peer, core_peer)):
+                start(spread(group, s, local, i, peer))
+
+    def wait_hidden(group, p):
+        for s in range(len(halves[group])):
+            spread(group, s, p, 0, core_peer).wait_recv()
 
     over_y0 = to_y(0)
     near0 = to_core(2, 0, core_peer_l)
@@ -149,6 +165,10 @@
         gather(1 - x, pz, fw_send.at[0], x_peer).wait_recv()
     over_y1 = to_y(1)
     gate0, up0 = partial_sums(0, local)
+
+    activate(0, *add_core(2, near0, gate0, up0), over_y0)
+    near1 = to_core(3, 1, core_peer_l)
+    gate1, up1 = partial_sums(1, local)
 
     loads[2].wait()
     loads[3].wait()
@@ -170,28 +190,27 @@
     for i, peer in enumerate(same_plane + other_plane):
         push(gates.at[x, z], gates.at[x, z], gate_send.at[i], gate_recv.at[x, z], peer)
 
-    activate(0, *add_core(2, near0, gate0, up0), over_y0)
-    near1 = to_core(3, 1, core_peer_l)
-    gate1, up1 = partial_sums(1, local)
-    activate(1, *add_core(3, near1, gate1, up1), over_y1)
-    loads[6].wait()
-
     chunk_at = [slice(j * cols, (j + 1) * cols) for j in range(CHUNKS)]
 
     def down(group, p, where):
         depth = pl.ds(pl.multiple_of(p * piece, piece), piece)
-        return jnp.dot(hid[group, p], dw[depth, where], preferred_element_type=f32)
+        units = jnp.concatenate([hid[p, group, 0], hid[p, group, 1]], axis=1)
+        return jnp.dot(units, dw[depth, where], preferred_element_type=f32)
 
     lane = lax.broadcasted_iota(jnp.int32, (half, LANES), 1)
     mine = (lane == node) | (lane == node + nodes) | (lane == node + 2 * nodes)
 
-    def give_back(group):
+    def begin_down(group):
         for where in chunk_at:
             acc[group, :, where] = down(group, local, where)
-        for p in (core_peer_l, y_peer_l):
-            spread(group, p, 0, core_peer).wait_recv()
-            for where in chunk_at:
-                acc[group, :, where] += down(group, p, where)
+        wait_hidden(group, core_peer_l)
+        for where in chunk_at:
+            acc[group, :, where] += down(group, core_peer_l, where)
+
+    def give_back(group):
+        wait_hidden(group, y_peer_l)
+        for where in chunk_at:
+            acc[group, :, where] += down(group, y_peer_l, where)
         for pz in z_peers + ([z] if group else []):
             pltpu.make_async_remote_copy(
                 src_ref=gates.at[x, z], dst_ref=gates.at[planes[group], pz], send_sem=gate_send.at[0],
@@ -199,7 +218,7 @@
             ).wait_recv()
         coded = gates[planes[group]].reshape(half, LANES).astype(f32)
         weight = jnp.sum(jnp.where(mine, coded, 0.0), axis=1, keepdims=True)
-        spread(group, far_l, 0, core_peer).wait_recv()
+        wait_hidden(group, far_l)
         targets = ([z] + z_peers, other_plane) if group else (z_peers, same_plane)
         for j, where in enumerate(chunk_at):
             result = (acc[group, :, where] + down(group, far_l, where)).astype(bf16).astype(f32)
@@ -213,7 +232,11 @@
                 push(back_out.at[group, j, pz], back_in.at[j, slot],
                      back_send.at[j, slot], back_recv.at[j, slot], peer)
 
+    loads[6].wait()
+    begin_down(0)
+    activate(1, *add_core(3, near1, gate1, up1), over_y1)
     give_back(0)
+    begin_down(1)
     give_back(1)
     for copy in sent:
         copy.wait_send()
@@ -256,17 +279,17 @@
             pltpu.VMEM((2, nz, rows, LANES), bf16),
             pltpu.VMEM((4, half, 2 * piece), bf16),
             pltpu.VMEM((4, half, 2 * piece), bf16),
-            pltpu.VMEM((2, half, 2 * piece), bf16),
-            pltpu.VMEM((2, half, 2 * piece), bf16),
-            pltpu.VMEM((2, 4, half, piece), bf16),
+            pltpu.VMEM((2, 2, half, piece), bf16),
+            pltpu.VMEM((2, 2, half, piece), bf16),
+            pltpu.VMEM((4, 2, 2, half, piece // 2), bf16),
             pltpu.VMEM((2, half, width), f32),
             pltpu.VMEM((CHUNKS, nz, rows, cols), f32),
             pltpu.VMEM((2, CHUNKS, nz, rows, cols), bf16),
             pltpu.VMEM((CHUNKS, nodes - 1, rows, cols), bf16),
             dma((7,)),
             dma((nz - 1,)), dma((2, nz)), dma((nz,)), dma((nodes - 1,)), dma((2, nz)),
-            dma((4,)), dma((4,)), dma((2,)), dma((2,)),
-            dma((2, 3)), dma((2, 4)),
+            dma((4,)), dma((4,)), dma((2, 2)), dma((2, 2)),
+            dma((2, 2, 3)), dma((2, 2, 4)),
             dma((CHUNKS, nodes - 1)), dma((CHUNKS, nodes - 1)),
         ],
         compiler_params=pltpu.CompilerParams(
@@ -287,7 +310,7 @@
         and rows % 16 == 0
         and nodes * rows <= 256
         and tokens.shape[1] % (CHUNKS * LANES) == 0
-        and gate_w.shape[2] % (4 * LANES) == 0
+        and gate_w.shape[2] % (8 * LANES) == 0
     )
 
 

time: 28.9 us -> 29.1 us (level)
  no operation moved by 1% of the time
where the time goes in v7:
time: 29.1 us; the launch traced here: 29 us
  Pallas kernels  28.3 us (97%)
  local copies, waits for them, and re-layouts  0.62 us (2%)
    pallas_call x1, Pallas kernels, fused(): pl.pallas_call(functools.partial(fused_kernel, nodes), out_shape=pltpu.VM...  28.3 us
    unnamed x1, local copies, waits for them, and re-layouts  0.62 us

profile of v7, /device:TPU:0, one launch (start us, length us, event | category | flops | bytes accessed | tf_op | source)
XLA Modules:
  0.0 29.0 jit_solution(15582971633507842241)
XLA Ops:
  0.0 28.3 %shard_map.73 = bf16[16,1024]{1,0:T(8,128)(2,1)S(1)} custom-call(bf16[16,1024]{1,0:T(8,128)(2,1)} %tok_hbm.1, s32[1,1024]{1,0:T(1,128)} %bitcast.3, s32[4,16]{1,0:T(4,128)} %bitcast.4, f32[4,16]{1,0:T(4,128)} %bitcast.5, bf16[1,1024,1024]{2,1,0:T(8,128)(2,1)} %gw_hbm.1, bf16[1,1024,1024]{2,1,0:T(8,128)(2,1)} %uw_hbm.1, bf16[1,1024,1024]{2,1,0:T(8,128)(2,1)} %dw_hbm.1), custom_call_target="tpu_custom_call" | custom-call | flops 805306368 | bytes 6291456 | tf_op jit(solution)/shard_map/pallas_call | solution.py:265
  28.3 0.6 %copy.9 = bf16[16,1024]{1,0:T(8,128)(2,1)} copy(bf16[16,1024]{1,0:T(8,128)(2,1)S(1)} %shard_map.73) | data formatting | bytes 65536

commit v8 on v4

--- a/solution.py
+++ b/solution.py
@@ -10,7 +10,7 @@
 
 HB = 128
 LANES = 128
-CHUNKS = 2
+CHUNKS = 1
 VMEM_BYTES = 63 * 1024 * 1024
 MESH = pl.DeviceIdType.MESH
 
@@ -20,7 +20,7 @@
     tok_hbm, sign_hbm, routes_hbm, gv_hbm, gw_hbm, uw_hbm, dw_hbm, out_ref,
     tok_ref, sign_ref, routes_ref, gv_ref, gw, uw, dw, arr,
     core_out, core_in, y_out, y_in, hid, acc, own, back_out, back_in,
-    w_sem, ag_send, ag_recv, fw_send, core_send, core_recv, y_send, y_recv,
+    w_sem, ag_send, ag_recv, fw_send, fw_recv, core_send, core_recv, y_send, y_recv,
     hid_send, hid_recv, back_send, back_recv,
 ):
     rows, width = tok_hbm.shape
@@ -62,13 +62,18 @@
     bits = bits ^ (bits >> 2)
     bits = bits ^ (bits >> 1)
     table = (1 - 2 * (bits & 1)).astype(f32).astype(bf16)
-    for load in loads[:4]:
-        load.wait()
+    loads[0].wait()
+    loads[1].wait()
     signs = (1 - 2 * sign_ref[...]).astype(f32)
     signed = (tok_ref[...].astype(f32) * signs).astype(bf16)
-    for b in range(width // HB):
-        block = jnp.dot(signed[:, b * HB : (b + 1) * HB], table, preferred_element_type=f32)
-        arr[x, z, :, b * HB : (b + 1) * HB] = (block * (1.0 / math.sqrt(HB))).astype(bf16)
+    count = width // HB
+    stacked = jnp.concatenate([signed[:, b * HB : (b + 1) * HB] for b in range(count)], axis=0)
+    turned = jnp.dot(stacked, table, preferred_element_type=f32) * (1.0 / math.sqrt(HB))
+    for b in range(count):
+        arr[x, z, :, b * HB : (b + 1) * HB] = turned[b * rows : (b + 1) * rows].astype(bf16)
+
+    loads[2].wait()
+    loads[3].wait()
     code = lax.broadcasted_iota(jnp.int32, (LANES, rows), 0)
     dense = jnp.zeros((LANES, rows), f32)
     for k in range(routes_ref.shape[0]):
@@ -87,32 +92,29 @@
 
     pl.semaphore_wait(barrier, len(peers))
 
-    def gather(plane, pz, send_sem, peer):
+    def gather(pz, send_sem, recv_sem, peer):
         return pltpu.make_async_remote_copy(
-            src_ref=arr.at[plane, pz], dst_ref=arr.at[plane, pz], send_sem=send_sem,
-            recv_sem=ag_recv.at[plane, pz], device_id=peer, device_id_type=MESH,
-        )
-
-    sent = []
-
-    def start(copy):
-        copy.start()
-        sent.append(copy)
-        return copy
+            src_ref=arr.at[x, pz], dst_ref=arr.at[x, pz], send_sem=send_sem,
+            recv_sem=recv_sem, device_id=peer, device_id_type=MESH,
+        )
+
+    def wait_all(ref, sem):
+        pltpu.make_async_copy(ref, ref, sem).wait()
 
     def push(src, dst, send_sem, recv_sem, peer):
-        return start(pltpu.make_async_remote_copy(
+        copy = pltpu.make_async_remote_copy(
             src_ref=src, dst_ref=dst, send_sem=send_sem, recv_sem=recv_sem,
             device_id=peer, device_id_type=MESH,
-        ))
+        )
+        copy.start()
+        return copy
 
     for i in (1, 2, 0):
-        start(gather(x, z, ag_send.at[i], same_plane[i]))
-    start(gather(x, z, fw_send.at[nz - 1], x_peer))
-    for i, pz in enumerate(z_peers):
-        copy = gather(x, pz, fw_send.at[i], x_peer)
-        copy.wait_recv()
-        start(copy)
+        gather(z, ag_send.at[0], ag_recv.at[z], same_plane[i]).start()
+    gather(z, fw_send.at[0], fw_recv.at[0], x_peer).start()
+    for pz in z_peers:
+        gather(pz, ag_send.at[0], ag_recv.at[pz], x_peer).wait_recv()
+        gather(pz, fw_send.at[0], fw_recv.at[0], x_peer).start()
     loads[4].wait()
     loads[5].wait()
 
@@ -129,7 +131,7 @@
         gate, up = partial_sums(group, p)
         core_out[i, :, :piece] = gate.astype(bf16)
         core_out[i, :, piece:] = up.astype(bf16)
-        return push(core_out.at[i], core_in.at[i], core_send.at[i], core_recv.at[i], core_peer)
+        return push(core_out.at[i], core_in.at[i], core_send.at[0], core_recv.at[i], core_peer)
 
     def add_core(i, copy, gate, up):
         copy.wait_recv()
@@ -140,11 +142,11 @@
         gate, up = add_core(group, copy, *partial_sums(group, y_peer_l))
         y_out[group, :, :piece] = gate.astype(bf16)
         y_out[group, :, piece:] = up.astype(bf16)
-        return push(y_out.at[group], y_in.at[group], y_send.at[group], y_recv.at[group], y_peer)
-
-    def spread(group, p, i, peer):
+        return push(y_out.at[group], y_in.at[group], y_send.at[0], y_recv.at[group], y_peer)
+
+    def spread(group, p, peer):
         return pltpu.make_async_remote_copy(
-            src_ref=hid.at[group, p], dst_ref=hid.at[group, p], send_sem=hid_send.at[group, i],
+            src_ref=hid.at[group, p], dst_ref=hid.at[group, p], send_sem=hid_send.at[group],
             recv_sem=hid_recv.at[group, p], device_id=peer, device_id_type=MESH,
         )
 
@@ -153,17 +155,17 @@
         gate = gate + y_in[group, :, :piece].astype(f32)
         up = up + y_in[group, :, piece:].astype(f32)
         hid[group, local] = (gate / (1.0 + jnp.exp(-gate)) * up).astype(bf16)
-        for i, peer in enumerate((y_peer, far_peer, core_peer)):
-            start(spread(group, local, i, peer))
+        for peer in (y_peer, far_peer, core_peer):
+            spread(group, local, peer).start()
 
     over_y0 = to_y(0)
     near0 = to_core(2, 0, core_peer_l)
-    for pz in [z] + z_peers:
-        gather(1 - x, pz, fw_send.at[0], x_peer).wait_recv()
+    wait_all(arr.at[1 - x], fw_recv.at[0])
     over_y1 = to_y(1)
     gate0, up0 = partial_sums(0, local)
+
+    activate(0, *add_core(2, near0, gate0, up0), over_y0)
     near1 = to_core(3, 1, core_peer_l)
-    activate(0, *add_core(2, near0, gate0, up0), over_y0)
     gate1, up1 = partial_sums(1, local)
     activate(1, *add_core(3, near1, gate1, up1), over_y1)
     loads[6].wait()
@@ -181,12 +183,12 @@
         for where in chunk_at:
             acc[group, :, where] = down(group, local, where)
         for p in (core_peer_l, y_peer_l):
-            spread(group, p, 0, core_peer).wait_recv()
+            spread(group, p, core_peer).wait_recv()
             for where in chunk_at:
                 acc[group, :, where] += down(group, p, where)
         coded = arr[planes[group], :, :, width:].reshape(half, LANES).astype(f32)
         weight = jnp.sum(jnp.where(mine, coded, 0.0), axis=1, keepdims=True)
-        spread(group, far_l, 0, core_peer).wait_recv()
+        spread(group, far_l, core_peer).wait_recv()
         targets = ([z] + z_peers, other_plane) if group else (z_peers, same_plane)
         for j, where in enumerate(chunk_at):
             result = (acc[group, :, where] + down(group, far_l, where)).astype(bf16).astype(f32)
@@ -194,23 +196,26 @@
             back_out[group, j] = weighted.astype(bf16)
             if group == 0:
                 own[j] = weighted
-            for i, (pz, peer) in enumerate(zip(*targets)):
+            for i in ((2, 3, 1, 0) if group else (1, 2, 0)):
+                pz, peer = targets[0][i], targets[1][i]
                 slot = i + group * (nz - 1)
                 push(back_out.at[group, j, pz], back_in.at[j, slot],
-                     back_send.at[j, slot], back_recv.at[j, slot], peer)
+                     back_send.at[0], back_recv.at[0], peer)
 
     give_back(0)
     give_back(1)
-    for copy in sent:
-        copy.wait_send()
+    wait_all(arr.at[x, : nz - 1], ag_send.at[0])
+    wait_all(arr.at[x], fw_send.at[0])
+    wait_all(core_out, core_send.at[0])
+    wait_all(y_out, y_send.at[0])
+    for group in range(2):
+        wait_all(hid.at[group, :3], hid_send.at[group])
+    wait_all(back_in, back_send.at[0])
+    wait_all(back_in, back_recv.at[0])
 
     for j, where in enumerate(chunk_at):
         mixed = own[j, z]
         for i in range(nodes - 1):
-            pltpu.make_async_remote_copy(
-                src_ref=back_out.at[0, j, 0], dst_ref=back_in.at[j, i], send_sem=back_send.at[j, i],
-                recv_sem=back_recv.at[j, i], device_id=x_peer, device_id_type=MESH,
-            ).wait_recv()
             mixed = mixed + back_in[j, i].astype(f32)
         out_ref[:, where] = mixed.astype(bf16)
 
@@ -249,10 +254,10 @@
             pltpu.VMEM((2, CHUNKS, nz, rows, cols), bf16),
             pltpu.VMEM((CHUNKS, nodes - 1, rows, cols), bf16),
             dma((7,)),
-            dma((nz - 1,)), dma((2, nz)), dma((nz,)),
-            dma((4,)), dma((4,)), dma((2,)), dma((2,)),
-            dma((2, 3)), dma((2, 4)),
-            dma((CHUNKS, nodes - 1)), dma((CHUNKS, nodes - 1)),
+            dma((1,)), dma((nz,)), dma((1,)), dma((1,)),
+            dma((1,)), dma((4,)), dma((1,)), dma((2,)),
+            dma((2,)), dma((2, 4)),
+            dma((1,)), dma((1,)),
         ],
         compiler_params=pltpu.CompilerParams(
             collective_id=0, has_side_effects=True, vmem_limit_bytes=VMEM_BYTES

time: 29 us -> 28.5 us (0.983)
  Pallas kernels: 28.2 us -> 27.8 us
    pallas_call x1, Pallas kernels: 28.2 us -> 27.8 us  [fused(): pl.pallas_call(functools.partial(fused_kernel, nodes), out_shape=pltpu.VM...]
where the time goes in v8:
time: 28.5 us; the launch traced here: 28.4 us
  Pallas kernels  27.8 us (98%)
  local copies, waits for them, and re-layouts  0.62 us (2%)
    pallas_call x1, Pallas kernels, fused(): pl.pallas_call(functools.partial(fused_kernel, nodes), out_shape=pltpu.VM...  27.8 us
    unnamed x1, local copies, waits for them, and re-layouts  0.62 us

profile of v8, /device:TPU:0, one launch (start us, length us, event | category | flops | bytes accessed | tf_op | source)
XLA Modules:
  0.0 28.4 jit_solution(3063377272055370003)
XLA Ops:
  0.0 27.8 %shard_map.73 = bf16[16,1024]{1,0:T(8,128)(2,1)S(1)} custom-call(bf16[16,1024]{1,0:T(8,128)(2,1)} %tok_hbm.1, s32[1,1024]{1,0:T(1,128)} %bitcast.3, s32[4,16]{1,0:T(4,128)} %bitcast.4, f32[4,16]{1,0:T(4,128)} %bitcast.5, bf16[1,1024,1024]{2,1,0:T(8,128)(2,1)} %gw_hbm.1, bf16[1,1024,1024]{2,1,0:T(8,128)(2,1)} %uw_hbm.1, bf16[1,1024,1024]{2,1,0:T(8,128)(2,1)} %dw_hbm.1), custom_call_target="tpu_custom_call" | custom-call | flops 805306368 | bytes 6291456 | tf_op jit(solution)/shard_map/pallas_call | solution.py:233
  27.8 0.6 %copy.9 = bf16[16,1024]{1,0:T(8,128)(2,1)} copy(bf16[16,1024]{1,0:T(8,128)(2,1)S(1)} %shard_map.73) | data formatting | bytes 65536

commit v9 on v8

--- a/solution.py
+++ b/solution.py
@@ -10,7 +10,7 @@
 
 HB = 128
 LANES = 128
-CHUNKS = 1
+SPLIT = 4
 VMEM_BYTES = 63 * 1024 * 1024
 MESH = pl.DeviceIdType.MESH
 
@@ -19,15 +19,15 @@
     nodes,
     tok_hbm, sign_hbm, routes_hbm, gv_hbm, gw_hbm, uw_hbm, dw_hbm, out_ref,
     tok_ref, sign_ref, routes_ref, gv_ref, gw, uw, dw, arr,
-    core_out, core_in, y_out, y_in, hid, acc, own, back_out, back_in,
+    core_out, core_in, y_out, y_in, hid, acc, own, back_out, back_in, lead_out, lead_in, pair_out, pair_in,
     w_sem, ag_send, ag_recv, fw_send, fw_recv, core_send, core_recv, y_send, y_recv,
-    hid_send, hid_recv, back_send, back_recv,
+    hid_send, hid_recv, back_send, back_recv, lead_send, lead_recv, pair_send, pair_recv,
 ):
     rows, width = tok_hbm.shape
     nz = nodes // 2
     half = nz * rows
     piece = gw.shape[1] // 4
-    cols = width // CHUNKS
+    lead = width // SPLIT
     f32, bf16 = jnp.float32, jnp.bfloat16
 
     node = lax.axis_index("node")
@@ -170,7 +170,7 @@
     activate(1, *add_core(3, near1, gate1, up1), over_y1)
     loads[6].wait()
 
-    chunk_at = [slice(j * cols, (j + 1) * cols) for j in range(CHUNKS)]
+    chunk_at = [slice(0, lead), slice(lead, width)]
 
     def down(group, p, where):
         depth = pl.ds(pl.multiple_of(p * piece, piece), piece)
@@ -192,18 +192,29 @@
         targets = ([z] + z_peers, other_plane) if group else (z_peers, same_plane)
         for j, where in enumerate(chunk_at):
             result = (acc[group, :, where] + down(group, far_l, where)).astype(bf16).astype(f32)
-            weighted = (result * weight).reshape(nz, rows, cols)
-            back_out[group, j] = weighted.astype(bf16)
+            weighted = (result * weight).reshape(nz, rows, -1)
             if group == 0:
-                own[j] = weighted
+                own[:, :, where] = weighted
+            if j == 0:
+                if group == 1:
+                    lead_out[...] = weighted.astype(bf16)
+                    push(lead_out, lead_in, lead_send.at[0], lead_recv.at[0], x_peer)
+                continue
+            back_out[group] = weighted.astype(bf16)
             for i in ((2, 3, 1, 0) if group else (1, 2, 0)):
                 pz, peer = targets[0][i], targets[1][i]
                 slot = i + group * (nz - 1)
-                push(back_out.at[group, j, pz], back_in.at[j, slot],
-                     back_send.at[0], back_recv.at[0], peer)
+                push(back_out.at[group, pz], back_in.at[slot], back_send.at[0], back_recv.at[0], peer)
 
     give_back(0)
     give_back(1)
+    wait_all(lead_in, lead_recv.at[0])
+    summed = own[:, :, :lead] + lead_in[...].astype(f32)
+    own[:, :, :lead] = summed
+    pair_out[...] = summed.astype(bf16)
+    for i in (1, 2, 0):
+        push(pair_out.at[z_peers[i]], pair_in.at[i], pair_send.at[0], pair_recv.at[0], same_plane[i])
+
     wait_all(arr.at[x, : nz - 1], ag_send.at[0])
     wait_all(arr.at[x], fw_send.at[0])
     wait_all(core_out, core_send.at[0])
@@ -211,12 +222,15 @@
     for group in range(2):
         wait_all(hid.at[group, :3], hid_send.at[group])
     wait_all(back_in, back_send.at[0])
+    wait_all(lead_out, lead_send.at[0])
+    wait_all(pair_in, pair_send.at[0])
     wait_all(back_in, back_recv.at[0])
-
-    for j, where in enumerate(chunk_at):
-        mixed = own[j, z]
-        for i in range(nodes - 1):
-            mixed = mixed + back_in[j, i].astype(f32)
+    wait_all(pair_in, pair_recv.at[0])
+
+    for where, parts_in in zip(chunk_at, (pair_in, back_in)):
+        mixed = own[z, :, where]
+        for i in range(parts_in.shape[0]):
+            mixed = mixed + parts_in[i].astype(f32)
         out_ref[:, where] = mixed.astype(bf16)
 
 
@@ -224,7 +238,7 @@
     nodes = lax.axis_size("node")
     rows, width = tokens.shape
     hidden = gate_w.shape[2]
-    nz, piece, cols = nodes // 2, hidden // 4, width // CHUNKS
+    nz, piece, cols = nodes // 2, hidden // 4, width - width // SPLIT
     total, half = nodes * rows, nz * rows
     bf16, f32 = jnp.bfloat16, jnp.float32
     dma = pltpu.SemaphoreType.DMA
@@ -250,14 +264,19 @@
             pltpu.VMEM((2, half, 2 * piece), bf16),
             pltpu.VMEM((2, 4, half, piece), bf16),
             pltpu.VMEM((2, half, width), f32),
-            pltpu.VMEM((CHUNKS, nz, rows, cols), f32),
-            pltpu.VMEM((2, CHUNKS, nz, rows, cols), bf16),
-            pltpu.VMEM((CHUNKS, nodes - 1, rows, cols), bf16),
+            pltpu.VMEM((nz, rows, width), f32),
+            pltpu.VMEM((2, nz, rows, cols), bf16),
+            pltpu.VMEM((nodes - 1, rows, cols), bf16),
+            pltpu.VMEM((nz, rows, width - cols), bf16),
+            pltpu.VMEM((nz, rows, width - cols), bf16),
+            pltpu.VMEM((nz, rows, width - cols), bf16),
+            pltpu.VMEM((nz - 1, rows, width - cols), bf16),
             dma((7,)),
             dma((1,)), dma((nz,)), dma((1,)), dma((1,)),
             dma((1,)), dma((4,)), dma((1,)), dma((2,)),
             dma((2,)), dma((2, 4)),
             dma((1,)), dma((1,)),
+            dma((1,)), dma((1,)), dma((1,)), dma((1,)),
         ],
         compiler_params=pltpu.CompilerParams(
             collective_id=0, has_side_effects=True, vmem_limit_bytes=VMEM_BYTES
@@ -276,7 +295,7 @@
         and lax.axis_size("local") == 4
         and rows % 16 == 0
         and nodes * rows <= 256
-        and tokens.shape[1] % (CHUNKS * LANES) == 0
+        and tokens.shape[1] % (SPLIT * LANES) == 0
         and gate_w.shape[2] % (4 * LANES) == 0
     )
 

time: 28.5 us -> 28.9 us (1.014)
  Pallas kernels: 27.8 us -> 28.1 us
    pallas_call x1, Pallas kernels: 27.8 us -> 28.1 us  [fused(): pl.pallas_call(functools.partial(fused_kernel, nodes), out_shape=pltpu.VM...]
where the time goes in v9:
time: 28.9 us; the launch traced here: 28.7 us
  Pallas kernels  28.1 us (97%)
  local copies, waits for them, and re-layouts  0.62 us (2%)
    pallas_call x1, Pallas kernels, fused(): pl.pallas_call(functools.partial(fused_kernel, nodes), out_shape=pltpu.VM...  28.1 us
    unnamed x1, local copies, waits for them, and re-layouts  0.62 us

profile of v9, /device:TPU:0, one launch (start us, length us, event | category | flops | bytes accessed | tf_op | source)
XLA Modules:
  0.0 28.7 jit_solution(812908526385962675)
XLA Ops:
  0.0 28.1 %shard_map.73 = bf16[16,1024]{1,0:T(8,128)(2,1)S(1)} custom-call(bf16[16,1024]{1,0:T(8,128)(2,1)} %tok_hbm.1, s32[1,1024]{1,0:T(1,128)} %bitcast.3, s32[4,16]{1,0:T(4,128)} %bitcast.4, f32[4,16]{1,0:T(4,128)} %bitcast.5, bf16[1,1024,1024]{2,1,0:T(8,128)(2,1)} %gw_hbm.1, bf16[1,1024,1024]{2,1,0:T(8,128)(2,1)} %uw_hbm.1, bf16[1,1024,1024]{2,1,0:T(8,128)(2,1)} %dw_hbm.1), custom_call_target="tpu_custom_call" | custom-call | flops 805306368 | bytes 6291456 | tf_op jit(solution)/shard_map/pallas_call | solution.py:247
  28.1 0.6 %copy.9 = bf16[16,1024]{1,0:T(8,128)(2,1)} copy(bf16[16,1024]{1,0:T(8,128)(2,1)S(1)} %shard_map.73) | data formatting | bytes 65536

commit v10 on v8

--- a/solution.py
+++ b/solution.py
@@ -34,7 +34,6 @@
     local = lax.axis_index("local")
     z, x = node // 2, node % 2
     y, c = local // 2, local % 2
-    x_peer = {"node": z * 2 + (1 - x)}
     z_peers = [z + 1 - 2 * (z % 2), (z + 2) % nz, nz - 1 - z]
     core_peer_l, y_peer_l, far_l = y * 2 + (1 - c), (1 - y) * 2 + c, (1 - y) * 2 + (1 - c)
     core_peer, y_peer, far_peer = {"local": core_peer_l}, {"local": y_peer_l}, {"local": far_l}
@@ -42,7 +41,7 @@
     other_plane = [{"node": pz * 2 + (1 - x)} for pz in [z] + z_peers]
 
     barrier = pltpu.get_barrier_semaphore()
-    peers = [core_peer, y_peer, x_peer] + same_plane
+    peers = [core_peer, y_peer] + same_plane + other_plane
     for peer in peers:
         pl.semaphore_signal(barrier, inc=1, device_id=peer, device_id_type=MESH)
 
@@ -92,11 +91,11 @@
 
     pl.semaphore_wait(barrier, len(peers))
 
-    def gather(pz, send_sem, recv_sem, peer):
-        return pltpu.make_async_remote_copy(
-            src_ref=arr.at[x, pz], dst_ref=arr.at[x, pz], send_sem=send_sem,
+    def gather(send_sem, recv_sem, peer):
+        pltpu.make_async_remote_copy(
+            src_ref=arr.at[x, z], dst_ref=arr.at[x, z], send_sem=send_sem,
             recv_sem=recv_sem, device_id=peer, device_id_type=MESH,
-        )
+        ).start()
 
     def wait_all(ref, sem):
         pltpu.make_async_copy(ref, ref, sem).wait()
@@ -110,11 +109,10 @@
         return copy
 
     for i in (1, 2, 0):
-        gather(z, ag_send.at[0], ag_recv.at[z], same_plane[i]).start()
-    gather(z, fw_send.at[0], fw_recv.at[0], x_peer).start()
-    for pz in z_peers:
-        gather(pz, ag_send.at[0], ag_recv.at[pz], x_peer).wait_recv()
-        gather(pz, fw_send.at[0], fw_recv.at[0], x_peer).start()
+        gather(ag_send.at[0], ag_recv.at[0], same_plane[i])
+    for i in (2, 3, 1, 0):
+        gather(fw_send.at[0], fw_recv.at[0], other_plane[i])
+    wait_all(arr.at[x, : nz - 1], ag_recv.at[0])
     loads[4].wait()
     loads[5].wait()
 
@@ -254,7 +252,7 @@
             pltpu.VMEM((2, CHUNKS, nz, rows, cols), bf16),
             pltpu.VMEM((CHUNKS, nodes - 1, rows, cols), bf16),
             dma((7,)),
-            dma((1,)), dma((nz,)), dma((1,)), dma((1,)),
+            dma((1,)), dma((1,)), dma((1,)), dma((1,)),
             dma((1,)), dma((4,)), dma((1,)), dma((2,)),
             dma((2,)), dma((2, 4)),
             dma((1,)), dma((1,)),

time: 28.5 us -> 29.7 us (1.042)
  Pallas kernels: 27.8 us -> 29 us
    pallas_call x1, Pallas kernels: 27.8 us -> 29 us  [fused(): pl.pallas_call(functools.partial(fused_kernel, nodes), out_shape=pltpu.VM...]
where the time goes in v10:
time: 29.7 us; the launch traced here: 29.6 us
  Pallas kernels  29 us (98%)
  local copies, waits for them, and re-layouts  0.62 us (2%)
    pallas_call x1, Pallas kernels, fused(): pl.pallas_call(functools.partial(fused_kernel, nodes), out_shape=pltpu.VM...  29 us
    unnamed x1, local copies, waits for them, and re-layouts  0.62 us

profile of v10, /device:TPU:0, one launch (start us, length us, event | category | flops | bytes accessed | tf_op | source)
XLA Modules:
  0.0 29.6 jit_solution(3718574326118237566)
XLA Ops:
  0.0 29.0 %shard_map.73 = bf16[16,1024]{1,0:T(8,128)(2,1)S(1)} custom-call(bf16[16,1024]{1,0:T(8,128)(2,1)} %tok_hbm.1, s32[1,1024]{1,0:T(1,128)} %bitcast.3, s32[4,16]{1,0:T(4,128)} %bitcast.4, f32[4,16]{1,0:T(4,128)} %bitcast.5, bf16[1,1024,1024]{2,1,0:T(8,128)(2,1)} %gw_hbm.1, bf16[1,1024,1024]{2,1,0:T(8,128)(2,1)} %uw_hbm.1, bf16[1,1024,1024]{2,1,0:T(8,128)(2,1)} %dw_hbm.1), custom_call_target="tpu_custom_call" | custom-call | flops 805306368 | bytes 6291456 | tf_op jit(solution)/shard_map/pallas_call | solution.py:231
  29.0 0.6 %copy.9 = bf16[16,1024]{1,0:T(8,128)(2,1)} copy(bf16[16,1024]{1,0:T(8,128)(2,1)S(1)} %shard_map.73) | data formatting | bytes 65536
